TPU v7x, 32 devices: a whole 2x2x4 slice. The times are simulated.
32 devices in a mesh: groups: 2 (over y), tensor: 8 (over z, x), dp: 2 (over core).
Axes of the slice: x: 2, y: 2, z: 4, core: 2. Of those that a mesh axis runs over, the one named last changes fastest.
Arguments:
- queries: bfloat16 [1024, 4096], P(('groups', 'dp', 'tensor')), parts along dimension 0, may hold values from -5 to 5
- token_key_rows: bfloat16 [1024, 512], P(('groups', 'dp', 'tensor')), parts along dimension 0, may hold values from -4.5 to 4.5
- token_value_rows: bfloat16 [1024, 512], P(('groups', 'dp', 'tensor')), parts along dimension 0, may hold values from -8 to 8
- stored_key_cache: bfloat16 [1024, 64, 512], P(('groups', 'dp', 'tensor')), parts along dimension 0, may hold values from -4.5 to 4.5
- stored_value_cache: bfloat16 [1024, 64, 512], P(('groups', 'dp', 'tensor')), parts along dimension 0, may hold values from -8 to 8
- cache_position_length: int32 [1024], P(('groups', 'dp', 'tensor')), parts along dimension 0, may hold values from 1 to 64, 16384 in all
- request_adapter_index: int32 [1024, 1], P(('groups', 'dp', 'tensor')), parts along dimension 0, may hold values from 0 to 7; in each aligned block of 32 rows (0 to 31, 32 to 63, ...) at most 4 rows name the same one
- adapter_slot_index: int32 [8], replicated, may hold values from 0 to 7, each once
- output_projection_weight: bfloat16 [4096, 8192], P('tensor'), may hold values from -0.09375 to 0.09375
- down_factor_weight: bfloat16 [8, 4096, 64], P('tensor'), may hold values from -0.09375 to 0.09375
- up_factor_weight: bfloat16 [8, 64, 8192], P('tensor'), may hold values from -0.75 to 0.75
Outputs:
- mixed: bfloat16 [1024, 8192], P(('groups', 'dp', 'tensor')), parts along dimension 0
There are 2 independent parts, one for each index of `groups`. A program takes and returns all parts, laid end to end along the dimension named above; an argument that names none is the same for every part. Nothing has to cross between parts.
Inputs may be any that keep to these rules, and one draw needn't show every extreme that they name: `request_adapter_index`: in the rows of one device (aligned blocks of 32 rows) no adapter is named by more than 4 requests; some block reaches 4. `adapter_slot_index`: A permutation of the adapters over slots; slot s lies on the device of tensor index s. `cache_position_length`: they sum to 16384 in each group; the longest is exactly 64.
All inputs are finite; a program needn't handle non-finite values.
Results may differ from a plain program's by a relative error of at most 0.013.
Values may be sent and summed in bfloat16 or wider, within the bound.
A program may use at most 128 MiB of HBM per device.

v0:
```python
import jax
import jax.numpy as jnp
from jax import lax
from jax.sharding import PartitionSpec as P

H = 32
KVH = 4
HD = 128
MOST = 4


def attend(
    queries,
    token_key_rows,
    token_value_rows,
    stored_key_cache,
    stored_value_cache,
    cache_position_length,
):
    req_count = queries.shape[0]
    cache_len = stored_key_cache.shape[1]
    per_group = H // KVH
    score_scale = HD ** (-0.5)
    query_heads = queries.reshape(req_count, KVH, per_group, HD)
    cached_keys = stored_key_cache.reshape(req_count, cache_len, KVH, HD)
    cached_values = stored_value_cache.reshape(req_count, cache_len, KVH, HD)
    fresh_keys = token_key_rows.reshape(req_count, KVH, HD)
    fresh_values = token_value_rows.astype(jnp.float32).reshape(req_count, KVH, HD)
    scores = (
        jnp.einsum("rkgd,rlkd->rkgl", query_heads, cached_keys, preferred_element_type=jnp.float32)
        * score_scale
    )
    fresh = (
        jnp.einsum("rkgd,rkd->rkg", query_heads, fresh_keys, preferred_element_type=jnp.float32)
        * score_scale
    )
    live = (jnp.arange(cache_len, dtype=jnp.int32)[None, :] < cache_position_length[:, None])[
        :, None, None, :
    ]
    row_top = jnp.maximum(jnp.max(jnp.where(live, scores, -1e30), axis=-1), fresh)
    weights = jnp.where(live, jnp.exp(scores - row_top[..., None]), 0.0)
    fresh_weight = jnp.exp(fresh - row_top)
    total = jnp.sum(weights, axis=-1) + fresh_weight
    probs = (weights / total[..., None]).astype(jnp.bfloat16)
    fresh_prob = (fresh_weight / total).astype(jnp.bfloat16)
    summed = jnp.einsum("rkgl,rlkd->rkgd", probs, cached_values, preferred_element_type=jnp.float32)
    summed = summed + fresh_prob.astype(jnp.float32)[..., None] * fresh_values[:, :, None, :]
    return summed.reshape(req_count, KVH * per_group * HD).astype(jnp.bfloat16)


def adapter_row_block(gathered_rows, down_factor_weight, up_factor_weight):
    flattened_rows = gathered_rows.reshape(-1, gathered_rows.shape[-1])
    reduced_rank_rows = jnp.dot(
        flattened_rows, down_factor_weight[0], preferred_element_type=jnp.float32
    ).astype(jnp.bfloat16)
    return jnp.dot(reduced_rank_rows, up_factor_weight[0], preferred_element_type=jnp.float32)


def on_device(
    queries,
    token_key_rows,
    token_value_rows,
    stored_key_cache,
    stored_value_cache,
    cache_position_length,
    request_adapter_index,
    adapter_slot_index,
    output_projection_weight,
    down_factor_weight,
    up_factor_weight,
):
    attn = attend(
        queries,
        token_key_rows,
        token_value_rows,
        stored_key_cache,
        stored_value_cache,
        cache_position_length,
    )
    row_count = attn.shape[0]
    width = attn.shape[1]
    peers = lax.axis_size("tensor")
    heads = lax.all_to_all(attn, "tensor", split_axis=1, concat_axis=0, tiled=True)
    adapter_count = adapter_slot_index.shape[0]
    home = jnp.sum(
        jnp.where(
            request_adapter_index == jnp.arange(adapter_count, dtype=jnp.int32)[None, :],
            adapter_slot_index[None, :],
            0,
        ),
        axis=1,
    )
    positions = jnp.arange(row_count, dtype=jnp.int32)
    same_home = (home[:, None] == home[None, :]) & (positions[:, None] > positions[None, :])
    rank_in_home = jnp.sum(same_home.astype(jnp.int32), axis=1)
    target = home * MOST + rank_in_home
    pick_mask = jnp.arange(peers * MOST, dtype=jnp.int32)[:, None] == target[None, :]
    pick = pick_mask.astype(jnp.bfloat16)
    outgoing = (
        jnp.dot(pick, attn, preferred_element_type=jnp.float32)
        .astype(jnp.bfloat16)
        .reshape(peers, MOST, width)
    )
    numbers = (positions + 1).astype(jnp.float32)
    tags = jnp.dot(pick_mask.astype(jnp.float32), numbers).astype(jnp.bfloat16).reshape(peers, MOST)
    arriving_rows, tag_in = (
        lax.all_to_all(outgoing, "tensor", split_axis=0, concat_axis=0, tiled=True),
        lax.all_to_all(tags, "tensor", split_axis=0, concat_axis=0, tiled=True),
    )
    adapter_update = adapter_row_block(arriving_rows, down_factor_weight, up_factor_weight)
    delta_high = adapter_update.astype(jnp.bfloat16)
    delta_rest = (adapter_update - delta_high.astype(jnp.float32)).astype(jnp.bfloat16)
    tag_int = tag_in.astype(jnp.int32)
    dest = jnp.arange(peers, dtype=jnp.int32)[:, None] * row_count + tag_int - 1
    dest = jnp.where(tag_int > 0, dest, -1).reshape(1, peers * MOST)
    place = (jnp.arange(peers * row_count, dtype=jnp.int32)[:, None] == dest).astype(jnp.bfloat16)
    projected = jnp.dot(heads, output_projection_weight, preferred_element_type=jnp.float32)
    high_part = jnp.dot(place, delta_high, preferred_element_type=jnp.float32)
    rest_part = jnp.dot(place, delta_rest, preferred_element_type=jnp.float32)
    summed = lax.psum_scatter(
        projected + (high_part + rest_part), "tensor", scatter_dimension=0, tiled=True
    )
    return summed.astype(jnp.bfloat16)


def solution(mesh):
    in_specs = (
        P(("groups", "dp", "tensor"), None),
        P(("groups", "dp", "tensor"), None),
        P(("groups", "dp", "tensor"), None),
        P(("groups", "dp", "tensor"), None, None),
        P(("groups", "dp", "tensor"), None, None),
        P(("groups", "dp", "tensor")),
        P(("groups", "dp", "tensor"), None),
        P(),
        P("tensor", None),
        P("tensor", None, None),
        P("tensor", None, None),
    )
    out_specs = P(("groups", "dp", "tensor"), None)
    return jax.shard_map(
        on_device, mesh=mesh, in_specs=in_specs, out_specs=out_specs, check_vma=False
    )
```

profile of v0, /device:TPU:0, one launch (start us, length us, event | category | flops | bytes accessed | tf_op | source)
XLA Modules:
  0.0 221.1 jit_solution(6355889754744139438)
XLA Ops:
  6.5 0.0 copy-start
  6.5 0.9 select_reduce_fusion.1
  7.4 0.2 convert_reduce_fusion
  7.6 0.1 fusion.17
  7.8 0.7 all_to_all.27
  8.5 7.3 %all-to-all-start.1 = ((bf16[8,1,4]{2,1,0:T(2,128)(2,1)}), bf16[8,1,4]{2,1,0:T(2,128)(2,1)S(1)}, u32[]{:S(2)}, u32[]{:S(2)}) async-start(bf16[8,1,4]{2,1,0:T(2,128)(2,1)} %all_to_all.27), calls=%async_computation.1 | async-start | bytes 8192 | tf_op jit(solution)/shard_map/all_to_all | solution.py:108
  15.7 0.1 add.51
  15.8 0.1 add.52
  15.9 0.7 iota_compare_fusion.7
  16.6 0.8 reshape.95
  17.4 0.8 reshape.88
  18.2 1.0 copy.29
  19.2 0.3 fusion.43
  19.4 2.9 %select_reduce_fusion = (f32[32,4,8]{2,1,0:T(4,128)S(1)}, f32[32,4,8,64]{3,2,1,0:T(8,128)S(1)}) fusion(pred[32,64]{1,0:T(8,128)(4,1)S(1)} %iota_compare_fusion.7, bf16[32,4,8,128]{3,2,1,0:T(8,128)(2,1)S(1)} %bitcast.60, bf16[32,64,512]{2,1,0:T(8,128)(2,1)} %param.14), kind=kOutput, calls=%fused_computation.21 | convolution fusion | flops 16972800 | bytes 2627584 | tf_op jit(solution)/shard_map/rkgd,rlkd->rkgl/dot_general | solution.py:30
  22.4 0.4 fusion.21
  22.8 0.1 fusion.35
  22.9 0.0 copy-done
  22.9 0.8 fusion.13
  23.6 0.2 convert_element_type.64
  23.8 0.8 copy.23
  24.6 0.0 all-to-all-done.1
  24.6 6.0 %all-to-all-start = ((bf16[32,8,512]{2,0,1:T(8,128)(2,1)}), bf16[32,8,512]{2,0,1:T(8,128)(2,1)S(1)}, u32[]{:S(2)}, u32[]{:S(2)}) async-start(bf16[32,8,512]{2,0,1:T(8,128)(2,1)} %copy.23), calls=%async_computation | async-start | bytes 524288 | tf_op jit(solution)/shard_map/all_to_all | solution.py:83
  30.6 0.2 convolution_convert_fusion
  30.8 0.8 reshape.86
  31.7 0.1 reshape.89
  31.7 7.4 %all-to-all-done = bf16[32,8,512]{2,0,1:T(8,128)(2,1)S(1)} async-done(((bf16[32,8,512]{2,0,1:T(8,128)(2,1)}), bf16[32,8,512]{2,0,1:T(8,128)(2,1)S(1)}, u32[]{:S(2)}, u32[]{:S(2)}) %all-to-all-start) | async-done | bytes 262176 | tf_op jit(solution)/shard_map/all_to_all | solution.py:83
  39.1 3.4 %all-to-all-start.2 = ((bf16[8,4,4096]{2,1,0:T(4,128)(2,1)}), bf16[8,4,4096]{2,1,0:T(4,128)(2,1)S(1)}, u32[]{:S(2)}, u32[]{:S(2)}) async-start(bf16[8,4,4096]{2,1,0:T(4,128)(2,1)} %reshape.86), calls=%async_computation.2 | async-start | bytes 524288 | tf_op jit(solution)/shard_map/all_to_all | solution.py:107
  42.5 0.0 reduce-scatter.2.cloned.1.call-start
  42.6 9.0 %fusion.44 = f32[256,8192]{1,0:T(8,128)} fusion(bf16[256,512]{1,0:T(8,128)(2,1)S(1)} %bitcast.58, bf16[512,8192]{1,0:T(8,128)(2,1)} %param.19), kind=kOutput, calls=%fused_computation.60 | convolution fusion | flops 2147483648 | bytes 17039360 | tf_op jit(solution)/shard_map/dot_general | solution.py:117
  51.5 0.0 all-to-all-done.2
  51.5 0.1 reshape.87
  51.6 2.2 fusion.16
  53.8 0.0 copy-start.1
  53.8 1.2 fusion.25
  55.0 2.2 copy-done.1
  57.2 4.5 %fusion = f32[256,8192]{1,0:T(8,128)} fusion(f32[256,8192]{1,0:T(8,128)S(1)} %copy-done.1, f32[256,8192]{1,0:T(8,128)S(1)} %fusion.25, f32[32,8192]{1,0:T(8,128)S(1)} %fusion.16, s32[32]{0:T(128)S(1)} %compare_select_fusion), kind=kOutput, calls=%fused_computation.1 | convolution fusion | flops 139468800 | bytes 26214528 | tf_op jit(solution)/shard_map/dot_general | solution.py:119
  61.6 0.0 reduce-scatter.2.cloned.1.call-update
  61.7 150.6 %reduce-scatter.2.cloned.1.call-done = f32[32,8192]{1,0:T(8,128)} async-done(((f32[256,8192]{1,0:T(8,128)}), f32[32,8192]{1,0:T(8,128)}) %reduce-scatter.2.cloned.1.call-update) | async-done | bytes 1048592 | tf_op jit(solution)/shard_map/reduce_scatter | solution.py:120
  212.2 2.1 convert_element_type.76
  (5 shorter events, 0.1 us)
Async XLA Ops:
  6.5 16.3 %copy-start = (bf16[32,64,512]{2,1,0:T(8,128)(2,1)S(1)}, bf16[32,64,512]{2,1,0:T(8,128)(2,1)}, u32[]{:S(2)}) copy-start(bf16[32,64,512]{2,1,0:T(8,128)(2,1)} %param.15) | copy-start | bytes 6291460
  8.5 16.1 %all-to-all-start.1 = ((bf16[8,1,4]{2,1,0:T(2,128)(2,1)}), bf16[8,1,4]{2,1,0:T(2,128)(2,1)S(1)}, u32[]{:S(2)}, u32[]{:S(2)}) async-start(bf16[8,1,4]{2,1,0:T(2,128)(2,1)} %all_to_all.27), calls=%async_computation.1 | async-start | bytes 8192 | tf_op jit(solution)/shard_map/all_to_all | solution.py:108
  24.6 14.5 %all-to-all-start = ((bf16[32,8,512]{2,0,1:T(8,128)(2,1)}), bf16[32,8,512]{2,0,1:T(8,128)(2,1)S(1)}, u32[]{:S(2)}, u32[]{:S(2)}) async-start(bf16[32,8,512]{2,0,1:T(8,128)(2,1)} %copy.23), calls=%async_computation | async-start | bytes 524288 | tf_op jit(solution)/shard_map/all_to_all | solution.py:83
  39.1 12.4 %all-to-all-start.2 = ((bf16[8,4,4096]{2,1,0:T(4,128)(2,1)}), bf16[8,4,4096]{2,1,0:T(4,128)(2,1)S(1)}, u32[]{:S(2)}, u32[]{:S(2)}) async-start(bf16[8,4,4096]{2,1,0:T(4,128)(2,1)} %reshape.86), calls=%async_computation.2 | async-start | bytes 524288 | tf_op jit(solution)/shard_map/all_to_all | solution.py:107
  42.5 169.7 %reduce-scatter.2.cloned.1.call-start = ((), (), s32[]{:S(2)}) async-start(), calls=%async_computation.4 | async-start | bytes 9437184 | tf_op jit(solution)/shard_map/reduce_scatter | solution.py:120
  53.8 3.4 %copy-start.1 = (f32[256,8192]{1,0:T(8,128)S(1)}, f32[256,8192]{1,0:T(8,128)}, u32[]{:S(2)}) copy-start(f32[256,8192]{1,0:T(8,128)} %fusion.44) | copy-start | bytes 25165828
Sparse Core Ops, SparseCore 0:
  61.8 150.4 reduce-scatter.1
where the time goes:
time: 222 us; the launch traced here: 221 us
  waiting for transfers between devices  158 us (71%)
  matrix products  21.1 us (10%)
  starting transfers between devices  16.7 us (8%)
  between operations  13.5 us (6%)
  local copies, waits for them, and re-layouts  7.47 us (3%)
  other arithmetic  4.45 us (2%)
    reduce_scatter x1, waiting for transfers between devices, on_device(): lax.psum_scatter(projected + (high_part + rest_part), 'tensor', scatter_d...  151 us
    dot_general x1, matrix products, on_device(): jnp.dot(heads, output_projection_weight, preferred_element_type=jnp.float32)  8.95 us
    all_to_all x1, waiting for transfers between devices, on_device(): lax.all_to_all(attn, 'tensor', split_axis=1, concat_axis=0, tiled=True)  7.37 us
    all_to_all x1, starting transfers between devices, on_device(): lax.all_to_all(tags, 'tensor', split_axis=0, concat_axis=0, tiled=True)  7.25 us
    all_to_all x1, starting transfers between devices, on_device(): lax.all_to_all(attn, 'tensor', split_axis=1, concat_axis=0, tiled=True)  5.99 us
    dot_general x1, matrix products, on_device(): rest_part = jnp.dot(place, delta_rest, preferred_element_type=jnp.float32)  4.47 us
  transfers between devices with their start and end apart: 4, of which 2 were waited for; matrix products, arithmetic and copies ran while one was open for 9% of the time, Pallas kernels for 0%

commit v1 on v0

--- a/solution.py
+++ b/solution.py
@@ -48,14 +48,6 @@
     return summed.reshape(req_count, KVH * per_group * HD).astype(jnp.bfloat16)
 
 
-def adapter_row_block(gathered_rows, down_factor_weight, up_factor_weight):
-    flattened_rows = gathered_rows.reshape(-1, gathered_rows.shape[-1])
-    reduced_rank_rows = jnp.dot(
-        flattened_rows, down_factor_weight[0], preferred_element_type=jnp.float32
-    ).astype(jnp.bfloat16)
-    return jnp.dot(reduced_rank_rows, up_factor_weight[0], preferred_element_type=jnp.float32)
-
-
 def on_device(
     queries,
     token_key_rows,
@@ -102,25 +94,24 @@
         .reshape(peers, MOST, width)
     )
     numbers = (positions + 1).astype(jnp.float32)
-    tags = jnp.dot(pick_mask.astype(jnp.float32), numbers).astype(jnp.bfloat16).reshape(peers, MOST)
-    arriving_rows, tag_in = (
-        lax.all_to_all(outgoing, "tensor", split_axis=0, concat_axis=0, tiled=True),
-        lax.all_to_all(tags, "tensor", split_axis=0, concat_axis=0, tiled=True),
+    tags = jnp.dot(pick_mask.astype(jnp.float32), numbers).astype(jnp.bfloat16)
+    tags = jnp.broadcast_to(tags.reshape(peers, MOST, 1), (peers, MOST, 128))
+    arriving = lax.all_to_all(
+        jnp.concatenate([outgoing, tags], axis=2), "tensor", split_axis=0, concat_axis=0, tiled=True
+    ).reshape(peers * MOST, width + 128)
+    low = jnp.dot(
+        arriving[:, :width], down_factor_weight[0], preferred_element_type=jnp.float32
+    ).astype(jnp.bfloat16)
+    tag_int = arriving[:, width].astype(jnp.int32)
+    base_row = (jnp.arange(peers * MOST, dtype=jnp.int32) // MOST) * row_count
+    dest = jnp.where(tag_int > 0, base_row + tag_int - 1, -1)[None, :]
+    place = (jnp.arange(peers * row_count, dtype=jnp.int32)[:, None] == dest).astype(jnp.bfloat16)
+    placed = jnp.dot(place, low, preferred_element_type=jnp.float32).astype(jnp.bfloat16)
+    projected = jnp.dot(heads, output_projection_weight, preferred_element_type=jnp.float32)
+    delta = jnp.dot(placed, up_factor_weight[0], preferred_element_type=jnp.float32)
+    return lax.psum_scatter(
+        (projected + delta).astype(jnp.bfloat16), "tensor", scatter_dimension=0, tiled=True
     )
-    adapter_update = adapter_row_block(arriving_rows, down_factor_weight, up_factor_weight)
-    delta_high = adapter_update.astype(jnp.bfloat16)
-    delta_rest = (adapter_update - delta_high.astype(jnp.float32)).astype(jnp.bfloat16)
-    tag_int = tag_in.astype(jnp.int32)
-    dest = jnp.arange(peers, dtype=jnp.int32)[:, None] * row_count + tag_int - 1
-    dest = jnp.where(tag_int > 0, dest, -1).reshape(1, peers * MOST)
-    place = (jnp.arange(peers * row_count, dtype=jnp.int32)[:, None] == dest).astype(jnp.bfloat16)
-    projected = jnp.dot(heads, output_projection_weight, preferred_element_type=jnp.float32)
-    high_part = jnp.dot(place, delta_high, preferred_element_type=jnp.float32)
-    rest_part = jnp.dot(place, delta_rest, preferred_element_type=jnp.float32)
-    summed = lax.psum_scatter(
-        projected + (high_part + rest_part), "tensor", scatter_dimension=0, tiled=True
-    )
-    return summed.astype(jnp.bfloat16)
 
 
 def solution(mesh):

time: 222 us -> 149 us (0.67)
  waiting for transfers between devices: 158 us -> 97 us
  starting transfers between devices: 16.7 us -> 10.9 us
  local copies, waits for them, and re-layouts: 7.47 us -> 3.85 us
    reduce_scatter x1, waiting for transfers between devices: 151 us -> 89.9 us  [on_device(): lax.psum_scatter((projected + delta).astype(jnp.bfloat16), 'tensor', scat...]
    all_to_all x2 -> x1, starting transfers between devices: 10.7 us -> 3.59 us  [on_device(): lax.all_to_all(jnp.concatenate([outgoing, tags], axis=2), 'tensor', split...]
    dot_general x4 -> x3, matrix products: 7.98 us -> 7.57 us  [the longest x1 7.18 us: on_device(): jnp.dot(placed, up_factor_weight[0], preferred_element_type=jnp.float32)]
  transfers between devices with their start and end apart: 4 -> 3, of which waited for: 2 -> 2; matrix products, arithmetic and copies ran while one was open for 9% -> 7% of each run, Pallas kernels for 0% -> 0%
where the time goes in v1:
time: 149 us
  waiting for transfers between devices  97 us (65%)
  matrix products  20.7 us (14%)
  between operations  13.5 us (9%)
  starting transfers between devices  10.9 us (7%)
  local copies, waits for them, and re-layouts  3.85 us (3%)
  other arithmetic  2.64 us (2%)
    reduce_scatter x1, waiting for transfers between devices, on_device(): lax.psum_scatter((projected + delta).astype(jnp.bfloat16), 'tensor', scat...  89.9 us
    dot_general x1, matrix products, on_device(): jnp.dot(heads, output_projection_weight, preferred_element_type=jnp.float32)  9.01 us
    all_to_all x1, starting transfers between devices, on_device(): lax.all_to_all(attn, 'tensor', split_axis=1, concat_axis=0, tiled=True)  7.25 us
    dot_general x1, matrix products, on_device(): jnp.dot(placed, up_factor_weight[0], preferred_element_type=jnp.float32)  7.18 us
    all_to_all x1, waiting for transfers between devices, on_device(): lax.all_to_all(attn, 'tensor', split_axis=1, concat_axis=0, tiled=True)  7.16 us
    all_to_all x1, starting transfers between devices, on_device(): lax.all_to_all(jnp.concatenate([outgoing, tags], axis=2), 'tensor', split...  3.59 us
  transfers between devices with their start and end apart: 3, of which 2 were waited for; matrix products, arithmetic and copies ran while one was open for 7% of the time, Pallas kernels for 0%

profile of v1, /device:TPU:0, one launch (start us, length us, event | category | flops | bytes accessed | tf_op | source)
XLA Modules:
  0.0 148.7 jit_solution(1960935868629976438)
XLA Ops:
  6.5 0.0 copy-start
  6.5 0.9 iota_compare_fusion.7
  7.4 0.8 reshape.95
  8.2 0.8 reshape.88
  9.0 1.0 copy.28
  10.0 0.3 fusion.42
  10.3 2.9 %select_reduce_fusion = (f32[32,4,8]{2,1,0:T(4,128)S(1)}, f32[32,4,8,64]{3,2,1,0:T(8,128)S(1)}) fusion(pred[32,64]{1,0:T(8,128)(4,1)S(1)} %iota_compare_fusion.7, bf16[32,4,8,128]{3,2,1,0:T(8,128)(2,1)S(1)} %bitcast.59, bf16[32,64,512]{2,1,0:T(8,128)(2,1)} %param.14), kind=kOutput, calls=%fused_computation.20 | convolution fusion | flops 16972800 | bytes 2627584 | tf_op jit(solution)/shard_map/rkgd,rlkd->rkgl/dot_general | solution.py:30
  13.2 0.4 fusion.19
  13.6 0.1 fusion.31
  13.7 0.0 copy-done
  13.7 0.0 copy-start.2
  13.7 0.0 copy-start.3
  13.7 0.7 fusion.13
  14.5 0.2 convert_element_type.58
  14.7 0.8 copy.23
  15.4 7.3 %all-to-all-start = ((bf16[32,8,512]{2,0,1:T(8,128)(2,1)}), bf16[32,8,512]{2,0,1:T(8,128)(2,1)S(1)}, u32[]{:S(2)}, u32[]{:S(2)}) async-start(bf16[32,8,512]{2,0,1:T(8,128)(2,1)} %copy.23), calls=%async_computation | async-start | bytes 524288 | tf_op jit(solution)/shard_map/all_to_all | solution.py:75
  22.7 0.0 copy-done.2
  22.7 0.0 copy-done.3
  22.7 0.1 select_reduce_fusion.1
  22.8 0.2 convert_reduce_fusion.1
  23.0 0.1 fusion.16
  23.1 0.1 broadcast_in_dim.60
  23.2 0.2 convolution_convert_fusion
  23.4 0.1 reshape.86
  23.5 0.1 broadcast_in_dim.61
  23.6 0.8 pad_maximum_fusion
  24.4 7.2 %all-to-all-done = bf16[32,8,512]{2,0,1:T(8,128)(2,1)S(1)} async-done(((bf16[32,8,512]{2,0,1:T(8,128)(2,1)}), bf16[32,8,512]{2,0,1:T(8,128)(2,1)S(1)}, u32[]{:S(2)}, u32[]{:S(2)}) %all-to-all-start) | async-done | bytes 262176 | tf_op jit(solution)/shard_map/all_to_all | solution.py:75
  31.6 3.6 %all-to-all-start.1 = ((bf16[8,4,4224]{2,1,0:T(4,128)(2,1)}), bf16[8,4,4224]{2,1,0:T(4,128)(2,1)S(1)}, u32[]{:S(2)}, u32[]{:S(2)}) async-start(bf16[8,4,4224]{2,1,0:T(4,128)(2,1)} %pad_maximum_fusion), calls=%async_computation.1 | async-start | bytes 540672 | tf_op jit(solution)/shard_map/all_to_all | solution.py:99
  35.2 0.0 reduce-scatter.2.cloned.1.call-start
  35.2 0.0 copy-start.1
  35.2 9.0 %fusion.43 = f32[256,8192]{1,0:T(8,128)} fusion(bf16[256,512]{1,0:T(8,128)(2,1)S(1)} %bitcast.57, bf16[512,8192]{1,0:T(8,128)(2,1)} %param.19), kind=kOutput, calls=%fused_computation.63 | convolution fusion | flops 2147483648 | bytes 17039360 | tf_op jit(solution)/shard_map/dot_general | solution.py:110
  44.3 0.0 all-to-all-done.1
  44.3 0.1 reshape.87
  44.3 0.1 convert_reduce_fusion
  44.4 0.0 copy-done.1
  44.5 0.3 convolution_convert_fusion.2
  44.7 7.2 %fusion = bf16[256,8192]{1,0:T(8,128)(2,1)} fusion(f32[256,8192]{1,0:T(8,128)} %fusion.43, bf16[32,64]{1,0:T(8,128)(2,1)S(1)} %convolution_convert_fusion.2, bf16[1,64,8192]{2,1,0:T(8,128)(2,1)} %param.21, s32[32]{0:T(128)S(1)} %compare_select_fusion), kind=kOutput, calls=%fused_computation.1 | convolution fusion | flops 273702912 | bytes 13635712 | tf_op jit(solution)/shard_map/dot_general | solution.py:111
  51.9 0.0 reduce-scatter.2.cloned.1.call-update
  51.9 89.9 %reduce-scatter.2.cloned.1.call-done = bf16[32,8192]{1,0:T(8,128)(2,1)} async-done(((bf16[256,8192]{1,0:T(8,128)(2,1)}), bf16[32,8192]{1,0:T(8,128)(2,1)}) %reduce-scatter.2.cloned.1.call-update) | async-done | bytes 524304 | tf_op jit(solution)/shard_map/reduce_scatter | solution.py:112
  (3 shorter events, 0.1 us)
Async XLA Ops:
  6.5 7.2 %copy-start = (bf16[32,64,512]{2,1,0:T(8,128)(2,1)S(1)}, bf16[32,64,512]{2,1,0:T(8,128)(2,1)}, u32[]{:S(2)}) copy-start(bf16[32,64,512]{2,1,0:T(8,128)(2,1)} %param.15) | copy-start | bytes 6291460
  13.7 9.0 %copy-start.2 = (s32[8]{0:T(128)S(1)}, s32[8]{0:T(128)}, u32[]{:S(2)}) copy-start(s32[8]{0:T(128)} %param.18) | copy-start | bytes 100
  13.7 9.0 %copy-start.3 = (s32[32,1]{0,1:T(1,128)S(1)}, s32[32,1]{0,1:T(1,128)}, u32[]{:S(2)}) copy-start(s32[32,1]{0,1:T(1,128)} %param.17) | copy-start | bytes 388
  15.4 16.2 %all-to-all-start = ((bf16[32,8,512]{2,0,1:T(8,128)(2,1)}), bf16[32,8,512]{2,0,1:T(8,128)(2,1)S(1)}, u32[]{:S(2)}, u32[]{:S(2)}) async-start(bf16[32,8,512]{2,0,1:T(8,128)(2,1)} %copy.23), calls=%async_computation | async-start | bytes 524288 | tf_op jit(solution)/shard_map/all_to_all | solution.py:75
  31.6 12.7 %all-to-all-start.1 = ((bf16[8,4,4224]{2,1,0:T(4,128)(2,1)}), bf16[8,4,4224]{2,1,0:T(4,128)(2,1)S(1)}, u32[]{:S(2)}, u32[]{:S(2)}) async-start(bf16[8,4,4224]{2,1,0:T(4,128)(2,1)} %pad_maximum_fusion), calls=%async_computation.1 | async-start | bytes 540672 | tf_op jit(solution)/shard_map/all_to_all | solution.py:99
  35.2 106.6 %reduce-scatter.2.cloned.1.call-start = ((), (), s32[]{:S(2)}) async-start(), calls=%async_computation.3 | async-start | bytes 4718592 | tf_op jit(solution)/shard_map/reduce_scatter | solution.py:112
  35.2 9.2 %copy-start.1 = (bf16[1,4096,64]{1,2,0:T(8,128)(2,1)S(1)}, bf16[1,4096,64]{1,2,0:T(8,128)(2,1)}, u32[]{:S(2)}) copy-start(bf16[1,4096,64]{1,2,0:T(8,128)(2,1)} %param.20) | copy-start | bytes 1572868
Sparse Core Ops, SparseCore 0:
  52.1 89.7 reduce-scatter.1

commit v2 on v1

--- a/solution.py
+++ b/solution.py
@@ -1,6 +1,10 @@
+import functools
+
 import jax
 import jax.numpy as jnp
 from jax import lax
+from jax.experimental import pallas as pl
+from jax.experimental.pallas import tpu as pltpu
 from jax.sharding import PartitionSpec as P
 
 H = 32
@@ -48,6 +52,171 @@
     return summed.reshape(req_count, KVH * per_group * HD).astype(jnp.bfloat16)
 
 
+CHUNKS = 8
+
+
+def project_kernel(
+    lines,
+    lhs_ref,
+    weight_ref,
+    up_ref,
+    out_ref,
+    weights,
+    pair_out,
+    pair_in,
+    line_out,
+    line_in,
+    own,
+    kept,
+    weight_sem,
+    up_sem,
+    pair_send,
+    pair_recv,
+    line_send,
+    line_recv,
+):
+    me = lax.axis_index("tensor")
+    line, side = me // 2, me % 2
+    other = 2 * line + (1 - side)
+    depth = weight_ref.shape[0]
+    rank = up_ref.shape[0]
+    rows = lhs_ref.shape[2]
+    span = pair_out.shape[3]
+
+    def columns(c):
+        return pl.ds(pl.multiple_of(c * span, span), span)
+
+    def weight_copy(c):
+        return pltpu.make_async_copy(
+            weight_ref.at[:, columns(c)], weights.at[c, pl.ds(0, depth)], weight_sem.at[c]
+        )
+
+    def up_copy(c):
+        return pltpu.make_async_copy(
+            up_ref.at[:, columns(c)], weights.at[c, pl.ds(depth, rank)], up_sem.at[c]
+        )
+
+    def pair_copy(c):
+        return pltpu.make_async_remote_copy(
+            src_ref=pair_out.at[c],
+            dst_ref=pair_in.at[c],
+            send_sem=pair_send.at[c],
+            recv_sem=pair_recv.at[c],
+            device_id={"tensor": other},
+            device_id_type=pl.DeviceIdType.MESH,
+        )
+
+    def line_copy(c, k):
+        to = (line + k) % lines
+        return pltpu.make_async_remote_copy(
+            src_ref=line_out.at[c, k],
+            dst_ref=line_in.at[c, k - 1],
+            send_sem=line_send.at[c, k - 1],
+            recv_sem=line_recv.at[c, k - 1],
+            device_id={"tensor": 2 * to + side},
+            device_id_type=pl.DeviceIdType.MESH,
+        )
+
+    @pl.loop(0, CHUNKS)
+    def _(c):
+        weight_copy(c).start()
+        up_copy(c).start()
+
+    barrier = pltpu.get_barrier_semaphore()
+    pl.semaphore_signal(
+        barrier, inc=1, device_id={"tensor": other}, device_id_type=pl.DeviceIdType.MESH
+    )
+    for k in range(1, lines):
+        pl.semaphore_signal(
+            barrier,
+            inc=1,
+            device_id={"tensor": 2 * ((line + k) % lines) + side},
+            device_id_type=pl.DeviceIdType.MESH,
+        )
+    pl.semaphore_wait(barrier, lines)
+
+    @pl.loop(0, CHUNKS)
+    def _(c):
+        weight_copy(c).wait()
+        up_copy(c).wait()
+        left = lhs_ref[:, 1 - side].reshape(lines * rows, depth + rank)
+        part = jnp.dot(left, weights[c], preferred_element_type=jnp.float32)
+        pair_out[c] = part.astype(jnp.bfloat16).reshape(lines, rows, span)
+        pair_copy(c).start()
+
+    @pl.loop(0, CHUNKS)
+    def _(c):
+        left = lhs_ref[:, side].reshape(lines * rows, depth + rank)
+        part = jnp.dot(left, weights[c], preferred_element_type=jnp.float32)
+        pair_own = part.reshape(lines, rows, span)
+        own[...] = pair_own
+        pair_copy(c).wait_recv()
+        for k in range(lines):
+            to = (line + k) % lines
+            both = own[to] + pair_in[c, to].astype(jnp.float32)
+            if k == 0:
+                kept[c] = both
+            else:
+                line_out[c, k] = both.astype(jnp.bfloat16)
+                line_copy(c, k).start()
+
+    @pl.loop(0, CHUNKS)
+    def _(c):
+        total = kept[c]
+        for k in range(1, lines):
+            line_copy(c, k).wait_recv()
+            total = total + line_in[c, k - 1].astype(jnp.float32)
+        out_ref[:, columns(c)] = total.astype(jnp.bfloat16)
+
+    @pl.loop(0, CHUNKS)
+    def _(c):
+        pair_copy(c).wait_send()
+        for k in range(1, lines):
+            line_copy(c, k).wait_send()
+
+
+def project_and_sum(lhs, weight, up, peers):
+    lines = peers // 2
+    rows = lhs.shape[0] // peers
+    depth, width = weight.shape
+    rank = up.shape[0]
+    span = width // CHUNKS
+    dma = pltpu.SemaphoreType.DMA
+    return pl.pallas_call(
+        functools.partial(project_kernel, lines),
+        out_shape=jax.ShapeDtypeStruct((rows, width), jnp.bfloat16),
+        in_specs=[
+            pl.BlockSpec(memory_space=pltpu.VMEM),
+            pl.BlockSpec(memory_space=pl.ANY),
+            pl.BlockSpec(memory_space=pl.ANY),
+        ],
+        out_specs=pl.BlockSpec(memory_space=pltpu.VMEM),
+        scratch_shapes=[
+            pltpu.VMEM((CHUNKS, depth + rank, span), jnp.bfloat16),
+            pltpu.VMEM((CHUNKS, lines, rows, span), jnp.bfloat16),
+            pltpu.VMEM((CHUNKS, lines, rows, span), jnp.bfloat16),
+            pltpu.VMEM((CHUNKS, lines, rows, span), jnp.bfloat16),
+            pltpu.VMEM((CHUNKS, lines - 1, rows, span), jnp.bfloat16),
+            pltpu.VMEM((lines, rows, span), jnp.float32),
+            pltpu.VMEM((CHUNKS, rows, span), jnp.float32),
+            dma((CHUNKS,)),
+            dma((CHUNKS,)),
+            dma((CHUNKS,)),
+            dma((CHUNKS,)),
+            dma((CHUNKS, lines - 1)),
+            dma((CHUNKS, lines - 1)),
+        ],
+        compiler_params=pltpu.CompilerParams(
+            collective_id=0, has_side_effects=True, vmem_limit_bytes=40 * 1024 * 1024
+        ),
+        cost_estimate=pl.CostEstimate(
+            flops=2 * lhs.shape[0] * (depth + rank) * width,
+            bytes_accessed=2 * (depth + rank) * width,
+            transcendentals=0,
+        ),
+    )(lhs.reshape(lines, 2, rows, depth + rank), weight, up)
+
+
 def on_device(
     queries,
     token_key_rows,
@@ -107,11 +276,8 @@
     dest = jnp.where(tag_int > 0, base_row + tag_int - 1, -1)[None, :]
     place = (jnp.arange(peers * row_count, dtype=jnp.int32)[:, None] == dest).astype(jnp.bfloat16)
     placed = jnp.dot(place, low, preferred_element_type=jnp.float32).astype(jnp.bfloat16)
-    projected = jnp.dot(heads, output_projection_weight, preferred_element_type=jnp.float32)
-    delta = jnp.dot(placed, up_factor_weight[0], preferred_element_type=jnp.float32)
-    return lax.psum_scatter(
-        (projected + delta).astype(jnp.bfloat16), "tensor", scatter_dimension=0, tiled=True
-    )
+    lhs = jnp.concatenate([heads, placed], axis=1)
+    return project_and_sum(lhs, output_projection_weight, up_factor_weight[0], peers)
 
 
 def solution(mesh):

time: 149 us -> 99.7 us (0.67)
  waiting for transfers between devices: 97 us -> 10.6 us
  Pallas kernels: 0 us -> 55.8 us
  matrix products: 20.7 us -> 5.84 us
  between operations: 13.5 us -> 0.18 us
  local copies, waits for them, and re-layouts: 3.85 us -> 10.9 us
  other arithmetic: 2.64 us -> 4.29 us
    reduce_scatter x1 -> x0, waiting for transfers between devices: 89.9 us -> none  [on_device(): lax.psum_scatter((projected + delta).astype(jnp.bfloat16), 'tensor', scat...]
    pallas_call x0 -> x1, Pallas kernels: none -> 55.8 us  [project_and_sum(): pl.pallas_call(functools.partial(project_kernel, lines), out_shape=jax.Sh...]
    dot_general x3 -> x1, matrix products: 16.5 us -> 1.6 us  [on_device(): jnp.dot(place, low, preferred_element_type=jnp.float32).astype(jnp.bfloat16)]
    all_to_all x1, waiting for transfers between devices: 0.01 us -> 5.56 us  [on_device(): lax.all_to_all(jnp.concatenate([outgoing, tags], axis=2), 'tensor', split...]
    unnamed x9 -> x16, local copies, waits for them, and re-layouts: 1.02 us -> 5.39 us
    all_to_all x1, starting transfers between devices: 3.59 us -> 7.38 us  [on_device(): lax.all_to_all(jnp.concatenate([outgoing, tags], axis=2), 'tensor', split...]
    all_to_all x1, starting transfers between devices: 7.25 us -> 4.04 us  [on_device(): lax.all_to_all(attn, 'tensor', split_axis=1, concat_axis=0, tiled=True)]
    convert_element_type x2, local copies, waits for them, and re-layouts: 0.94 us -> 3.53 us  [attend(): return summed.reshape(req_count, KVH * per_group * HD).astype(jnp.bfloat16)]
  transfers between devices with their start and end apart: 3 -> 2, of which waited for: 2 -> 2; matrix products, arithmetic and copies ran while one was open for 7% -> 7% of each run, Pallas kernels for 0% -> 0%
where the time goes in v2:
time: 99.7 us; the launch traced here: 99 us
  Pallas kernels  55.8 us (56%)
  starting transfers between devices  11.4 us (11%)
  local copies, waits for them, and re-layouts  10.9 us (11%)
  waiting for transfers between devices  10.6 us (11%)
  matrix products  5.84 us (6%)
  other arithmetic  4.29 us (4%)
    pallas_call x1, Pallas kernels, project_and_sum(): pl.pallas_call(functools.partial(project_kernel, lines), out_shape=jax.Sh...  55.8 us
    all_to_all x1, starting transfers between devices, on_device(): lax.all_to_all(jnp.concatenate([outgoing, tags], axis=2), 'tensor', split...  7.38 us
    all_to_all x1, waiting for transfers between devices, on_device(): lax.all_to_all(jnp.concatenate([outgoing, tags], axis=2), 'tensor', split...  5.56 us
    unnamed x16, local copies, waits for them, and re-layouts  5.39 us
    all_to_all x1, waiting for transfers between devices, on_device(): lax.all_to_all(attn, 'tensor', split_axis=1, concat_axis=0, tiled=True)  5.04 us
    all_to_all x1, starting transfers between devices, on_device(): lax.all_to_all(attn, 'tensor', split_axis=1, concat_axis=0, tiled=True)  4.04 us
    convert_element_type x2, local copies, waits for them, and re-layouts, attend(): return summed.reshape(req_count, KVH * per_group * HD).astype(jnp.bfloat16)  3.53 us
    dot_general x1, matrix products, attend(): jnp.einsum('rkgd,rlkd->rkgl', query_heads, cached_keys, preferred_element...  2.89 us
  transfers between devices with their start and end apart: 2, of which 2 were waited for; matrix products, arithmetic and copies ran while one was open for 7% of the time, Pallas kernels for 0%

profile of v2, /device:TPU:0, one launch (start us, length us, event | category | flops | bytes accessed | tf_op | source)
XLA Modules:
  0.0 99.0 jit_solution(3376554133547700460)
XLA Ops:
  0.0 0.0 copy-start
  0.0 0.9 iota_compare_fusion.6
  0.9 1.0 %copy.33 = bf16[4,8,32,128]{3,2,1,0:T(8,128)(2,1)S(1)} copy(bf16[4,8,32,128]{3,1,2,0:T(8,128)(2,1)} %bitcast.61) | data formatting | bytes 524288
  1.9 0.8 reshape.99
  2.7 0.3 fusion.41
  2.9 0.0 copy-start.4
  3.0 0.0 copy-start.5
  3.0 0.0 copy-start.6
  3.0 2.9 %select_reduce_fusion = (f32[32,4,8]{2,1,0:T(4,128)S(1)}, f32[32,4,8,64]{3,2,1,0:T(8,128)S(1)}) fusion(pred[32,64]{1,0:T(8,128)(4,1)S(1)} %iota_compare_fusion.6, bf16[32,4,8,128]{3,2,1,0:T(8,128)(2,1)S(1)} %bitcast.56, bf16[32,64,512]{2,1,0:T(8,128)(2,1)} %param.14), kind=kOutput, calls=%fused_computation.17 | convolution fusion | flops 16972800 | bytes 2627584 | tf_op jit(solution)/shard_map/rkgd,rlkd->rkgl/dot_general | solution.py:34
  5.9 0.4 fusion.18
  6.4 0.1 fusion.30
  6.4 0.0 copy-done.4
  6.5 0.0 copy-done.5
  6.5 0.0 copy-done.6
  6.5 0.1 select_reduce_fusion.1
  6.6 0.2 convert_reduce_fusion.1
  6.7 0.1 fusion.15
  6.9 0.0 copy-done
  6.9 0.7 fusion.12
  7.6 0.0 copy-start.3
  7.6 0.2 convolution_convert_fusion
  7.8 0.1 reshape.90
  8.0 0.1 broadcast_in_dim.60
  8.0 0.1 broadcast_in_dim.61
  8.1 0.2 copy-done.3
  8.3 0.8 pad_maximum_fusion.1
  9.1 0.0 copy-start.2
  9.1 7.4 %all-to-all-start.1 = ((bf16[8,4,4224]{2,1,0:T(4,128)(2,1)}), bf16[8,4,4224]{2,1,0:T(4,128)(2,1)S(1)}, u32[]{:S(2)}, u32[]{:S(2)}) async-start(bf16[8,4,4224]{2,1,0:T(4,128)(2,1)} %pad_maximum_fusion.1), calls=%async_computation.1 | async-start | bytes 540672 | tf_op jit(solution)/shard_map/all_to_all | solution.py:268
  16.5 1.8 %convert_element_type.55 = bf16[32,8,512]{2,1,0:T(8,128)(2,1)} reshape(bf16[32,4,8,128]{3,2,1,0:T(8,128)(2,1)} %copy-done.3) | data formatting | bytes 524288 | tf_op jit(solution)/shard_map/convert_element_type | solution.py:52
  18.3 1.7 %copy.27 = bf16[32,8,512]{2,0,1:T(8,128)(2,1)} copy(bf16[32,8,512]{2,1,0:T(8,128)(2,1)} %convert_element_type.55) | data formatting | bytes 524288 | tf_op jit(solution)/shard_map/convert_element_type | solution.py:52
  20.1 5.6 %all-to-all-done.1 = bf16[8,4,4224]{2,1,0:T(4,128)(2,1)S(1)} async-done(((bf16[8,4,4224]{2,1,0:T(4,128)(2,1)}), bf16[8,4,4224]{2,1,0:T(4,128)(2,1)S(1)}, u32[]{:S(2)}, u32[]{:S(2)}) %all-to-all-start.1) | async-done | bytes 270368 | tf_op jit(solution)/shard_map/all_to_all | solution.py:268
  25.6 4.0 %all-to-all-start = ((bf16[32,8,512]{2,0,1:T(8,128)(2,1)}), bf16[32,8,512]{2,0,1:T(8,128)(2,1)}, u32[]{:S(2)}, u32[]{:S(2)}) async-start(bf16[32,8,512]{2,0,1:T(8,128)(2,1)} %copy.27), calls=%async_computation | async-start | bytes 524288 | tf_op jit(solution)/shard_map/all_to_all | solution.py:244
  29.7 0.8 reshape.91
  30.4 0.8 convert_reduce_fusion
  31.3 1.6 %convolution_convert_fusion.1 = bf16[256,64]{0,1:T(8,128)(2,1)S(1)} fusion(bf16[1,4096,64]{1,2,0:T(8,128)(2,1)} %param.20, bf16[32,4224]{1,0:T(8,128)(2,1)} %reshape.91, s32[32]{0:T(128)S(1)} %compare_select_fusion), kind=kOutput, calls=%fused_computation.10 | convolution fusion | flops 17852416 | bytes 819328 | tf_op jit(solution)/shard_map/dot_general | solution.py:278
  32.9 0.1 copy.28
  33.0 5.0 %all-to-all-done = bf16[32,8,512]{2,0,1:T(8,128)(2,1)} async-done(((bf16[32,8,512]{2,0,1:T(8,128)(2,1)}), bf16[32,8,512]{2,0,1:T(8,128)(2,1)}, u32[]{:S(2)}, u32[]{:S(2)}) %all-to-all-start) | async-done | bytes 262176 | tf_op jit(solution)/shard_map/all_to_all | solution.py:244
  38.0 1.0 pad_maximum_fusion.lhs_ref
  39.0 0.0 copy-done.2
  39.0 0.0 copy-start.1
  39.0 3.4 %copy-done.1 = bf16[512,8192]{1,0:T(8,128)(2,1)S(1)} copy-done((bf16[512,8192]{1,0:T(8,128)(2,1)S(1)}, bf16[512,8192]{1,0:T(8,128)(2,1)}, u32[]{:S(2)}) %copy-start.1) | copy-done | bytes 8388632
  42.4 55.8 %shard_map.109 = bf16[32,8192]{1,0:T(8,128)(2,1)S(1)} custom-call(bf16[4,2,32,576]{3,2,1,0:T(8,128)(2,1)S(1)} %pad_maximum_fusion.lhs_ref, bf16[512,8192]{1,0:T(8,128)(2,1)S(1)} %copy-done.1, bf16[64,8192]{1,0:T(8,128)(2,1)S(1)} %bitcast.54), custom_call_target="tpu_custom_call" | custom-call | flops 2415919104 | bytes 9437184 | tf_op jit(solution)/shard_map/pallas_call | solution.py:185
  98.2 0.8 copy.56
  (4 shorter events, 0.1 us)
Async XLA Ops:
  0.0 6.9 %copy-start = (bf16[32,64,512]{2,1,0:T(8,128)(2,1)S(1)}, bf16[32,64,512]{2,1,0:T(8,128)(2,1)}, u32[]{:S(2)}) copy-start(bf16[32,64,512]{2,1,0:T(8,128)(2,1)} %param.15) | copy-start | bytes 6291460
  2.9 3.5 %copy-start.4 = (bf16[32,512]{1,0:T(8,128)(2,1)S(1)}, bf16[32,512]{1,0:T(8,128)(2,1)}, u32[]{:S(2)}) copy-start(bf16[32,512]{1,0:T(8,128)(2,1)} %param.13) | copy-start | bytes 98308
  3.0 3.5 %copy-start.5 = (s32[8]{0:T(128)S(1)}, s32[8]{0:T(128)}, u32[]{:S(2)}) copy-start(s32[8]{0:T(128)} %param.18) | copy-start | bytes 100
  3.0 3.5 %copy-start.6 = (s32[32,1]{0,1:T(1,128)S(1)}, s32[32,1]{0,1:T(1,128)}, u32[]{:S(2)}) copy-start(s32[32,1]{0,1:T(1,128)} %param.17) | copy-start | bytes 388
  7.6 0.7 copy-start.3
  9.1 29.9 %copy-start.2 = (bf16[1,64,8192]{2,1,0:T(8,128)(2,1)S(1)}, bf16[1,64,8192]{2,1,0:T(8,128)(2,1)}, u32[]{:S(2)}) copy-start(bf16[1,64,8192]{2,1,0:T(8,128)(2,1)} %param.21) | copy-start | bytes 3145732
  9.1 16.5 %all-to-all-start.1 = ((bf16[8,4,4224]{2,1,0:T(4,128)(2,1)}), bf16[8,4,4224]{2,1,0:T(4,128)(2,1)S(1)}, u32[]{:S(2)}, u32[]{:S(2)}) async-start(bf16[8,4,4224]{2,1,0:T(4,128)(2,1)} %pad_maximum_fusion.1), calls=%async_computation.1 | async-start | bytes 540672 | tf_op jit(solution)/shard_map/all_to_all | solution.py:268
  25.6 12.4 %all-to-all-start = ((bf16[32,8,512]{2,0,1:T(8,128)(2,1)}), bf16[32,8,512]{2,0,1:T(8,128)(2,1)}, u32[]{:S(2)}, u32[]{:S(2)}) async-start(bf16[32,8,512]{2,0,1:T(8,128)(2,1)} %copy.27), calls=%async_computation | async-start | bytes 524288 | tf_op jit(solution)/shard_map/all_to_all | solution.py:244
  39.0 3.4 %copy-start.1 = (bf16[512,8192]{1,0:T(8,128)(2,1)S(1)}, bf16[512,8192]{1,0:T(8,128)(2,1)}, u32[]{:S(2)}) copy-start(bf16[512,8192]{1,0:T(8,128)(2,1)} %weight_ref.1) | copy-start | bytes 25165828

commit v3 on v2

--- a/solution.py
+++ b/solution.py
@@ -57,10 +57,16 @@
 
 def project_kernel(
     lines,
-    lhs_ref,
+    attn_ref,
+    target_row_ref,
+    target_column_ref,
+    down_ref,
     weight_ref,
     up_ref,
     out_ref,
+    outbox,
+    inbox,
+    lhs_ref,
     weights,
     pair_out,
     pair_in,
@@ -68,6 +74,8 @@
     line_in,
     own,
     kept,
+    mail_send,
+    mail_recv,
     weight_sem,
     up_sem,
     pair_send,
@@ -82,6 +90,9 @@
     rank = up_ref.shape[0]
     rows = lhs_ref.shape[2]
     span = pair_out.shape[3]
+    peers = 2 * lines
+    blocks = rows // MOST
+    block = attn_ref.shape[1] // blocks
 
     def columns(c):
         return pl.ds(pl.multiple_of(c * span, span), span)
@@ -94,6 +105,17 @@
     def up_copy(c):
         return pltpu.make_async_copy(
             up_ref.at[:, columns(c)], weights.at[c, pl.ds(depth, rank)], up_sem.at[c]
+        )
+
+    def mail_copy(k):
+        to = (me + k) % peers
+        return pltpu.make_async_remote_copy(
+            src_ref=outbox.at[to],
+            dst_ref=inbox.at[me],
+            send_sem=mail_send.at[k - 1],
+            recv_sem=mail_recv.at[k - 1],
+            device_id={"tensor": to},
+            device_id_type=pl.DeviceIdType.MESH,
         )
 
     def pair_copy(c):
@@ -123,17 +145,59 @@
         up_copy(c).start()
 
     barrier = pltpu.get_barrier_semaphore()
-    pl.semaphore_signal(
-        barrier, inc=1, device_id={"tensor": other}, device_id_type=pl.DeviceIdType.MESH
-    )
-    for k in range(1, lines):
+    for k in range(1, peers):
         pl.semaphore_signal(
             barrier,
             inc=1,
-            device_id={"tensor": 2 * ((line + k) % lines) + side},
+            device_id={"tensor": (me + k) % peers},
             device_id_type=pl.DeviceIdType.MESH,
         )
-    pl.semaphore_wait(barrier, lines)
+
+    for p in range(peers):
+        outbox[p, :, :depth] = attn_ref[:, p * depth : (p + 1) * depth]
+    picked_shape = (peers * rows, rows)
+    spot = lax.broadcasted_iota(jnp.int32, picked_shape, 0)
+    wanted = (spot // rows) * MOST + (spot % rows) // blocks
+    match = wanted == jnp.broadcast_to(target_row_ref[...], picked_shape)
+    picked = jnp.zeros((peers * rows, block), jnp.float32)
+    for b in range(blocks):
+        pick = jnp.where(match & (spot % blocks == b), 1.0, 0.0).astype(jnp.bfloat16)
+        picked = picked + jnp.dot(
+            pick,
+            attn_ref[:, b * block : (b + 1) * block],
+            preferred_element_type=jnp.float32,
+        )
+    outbox[:, :, depth : depth + block] = picked.astype(jnp.bfloat16).reshape(peers, rows, block)
+    target = jnp.broadcast_to(target_column_ref[...], (rows, 128))
+    lane = lax.broadcasted_iota(jnp.int32, (rows, 128), 1)
+    for p in range(peers):
+        here = (target // MOST == p) & (lane == me * MOST + target % MOST)
+        outbox[p, :, depth + block :] = jnp.where(here, 1.0, 0.0).astype(jnp.bfloat16)
+    pl.semaphore_wait(barrier, peers - 1)
+    for k in range(1, peers):
+        mail_copy(k).start()
+    inbox[me] = outbox[me]
+    for k in range(1, peers):
+        mail_copy(k).wait_recv()
+
+    arrived = inbox[:, :, depth : depth + block].reshape(peers * rows, block)
+    spot = lax.broadcasted_iota(jnp.int32, (peers * rows, rank), 0)
+    low = jnp.zeros((peers * rows, rank), jnp.float32)
+    for b in range(blocks):
+        term = lax.dot_general(
+            arrived,
+            down_ref[:, b * block : (b + 1) * block],
+            (((1,), (1,)), ((), ())),
+            preferred_element_type=jnp.float32,
+        )
+        low = low + jnp.where(spot % blocks == b, term, 0.0)
+    low = jnp.sum(low.reshape(peers * MOST, blocks, rank), axis=1)
+    low = jnp.concatenate([low, jnp.zeros((128 - peers * MOST, rank), jnp.float32)], axis=0)
+    place = inbox[:, :, depth + block :].reshape(peers * rows, 128)
+    placed = jnp.dot(place, low.astype(jnp.bfloat16), preferred_element_type=jnp.float32)
+    placed = placed.astype(jnp.bfloat16).reshape(lines, 2, rows, rank)
+    lhs_ref[:, :, :, :depth] = inbox[:, :, :depth].reshape(lines, 2, rows, depth)
+    lhs_ref[:, :, :, depth:] = placed
 
     @pl.loop(0, CHUNKS)
     def _(c):
@@ -174,24 +238,34 @@
         for k in range(1, lines):
             line_copy(c, k).wait_send()
 
-
-def project_and_sum(lhs, weight, up, peers):
+    for k in range(1, peers):
+        mail_copy(k).wait_send()
+
+
+def project_and_sum(attn, target, down, weight, up, peers):
     lines = peers // 2
-    rows = lhs.shape[0] // peers
+    rows = attn.shape[0]
     depth, width = weight.shape
     rank = up.shape[0]
     span = width // CHUNKS
+    letter = depth + MOST * attn.shape[1] // rows + 128
     dma = pltpu.SemaphoreType.DMA
     return pl.pallas_call(
         functools.partial(project_kernel, lines),
         out_shape=jax.ShapeDtypeStruct((rows, width), jnp.bfloat16),
         in_specs=[
             pl.BlockSpec(memory_space=pltpu.VMEM),
+            pl.BlockSpec(memory_space=pltpu.VMEM),
+            pl.BlockSpec(memory_space=pltpu.VMEM),
+            pl.BlockSpec(memory_space=pltpu.VMEM),
             pl.BlockSpec(memory_space=pl.ANY),
             pl.BlockSpec(memory_space=pl.ANY),
         ],
         out_specs=pl.BlockSpec(memory_space=pltpu.VMEM),
         scratch_shapes=[
+            pltpu.VMEM((peers, rows, letter), jnp.bfloat16),
+            pltpu.VMEM((peers, rows, letter), jnp.bfloat16),
+            pltpu.VMEM((lines, 2, rows, depth + rank), jnp.bfloat16),
             pltpu.VMEM((CHUNKS, depth + rank, span), jnp.bfloat16),
             pltpu.VMEM((CHUNKS, lines, rows, span), jnp.bfloat16),
             pltpu.VMEM((CHUNKS, lines, rows, span), jnp.bfloat16),
@@ -199,6 +273,8 @@
             pltpu.VMEM((CHUNKS, lines - 1, rows, span), jnp.bfloat16),
             pltpu.VMEM((lines, rows, span), jnp.float32),
             pltpu.VMEM((CHUNKS, rows, span), jnp.float32),
+            dma((peers - 1,)),
+            dma((peers - 1,)),
             dma((CHUNKS,)),
             dma((CHUNKS,)),
             dma((CHUNKS,)),
@@ -210,11 +286,11 @@
             collective_id=0, has_side_effects=True, vmem_limit_bytes=40 * 1024 * 1024
         ),
         cost_estimate=pl.CostEstimate(
-            flops=2 * lhs.shape[0] * (depth + rank) * width,
+            flops=2 * peers * rows * (depth + rank) * width,
             bytes_accessed=2 * (depth + rank) * width,
             transcendentals=0,
         ),
-    )(lhs.reshape(lines, 2, rows, depth + rank), weight, up)
+    )(attn, target.reshape(1, rows), target.reshape(rows, 1), down.T, weight, up)
 
 
 def on_device(
@@ -239,9 +315,7 @@
         cache_position_length,
     )
     row_count = attn.shape[0]
-    width = attn.shape[1]
     peers = lax.axis_size("tensor")
-    heads = lax.all_to_all(attn, "tensor", split_axis=1, concat_axis=0, tiled=True)
     adapter_count = adapter_slot_index.shape[0]
     home = jnp.sum(
         jnp.where(
@@ -255,29 +329,14 @@
     same_home = (home[:, None] == home[None, :]) & (positions[:, None] > positions[None, :])
     rank_in_home = jnp.sum(same_home.astype(jnp.int32), axis=1)
     target = home * MOST + rank_in_home
-    pick_mask = jnp.arange(peers * MOST, dtype=jnp.int32)[:, None] == target[None, :]
-    pick = pick_mask.astype(jnp.bfloat16)
-    outgoing = (
-        jnp.dot(pick, attn, preferred_element_type=jnp.float32)
-        .astype(jnp.bfloat16)
-        .reshape(peers, MOST, width)
-    )
-    numbers = (positions + 1).astype(jnp.float32)
-    tags = jnp.dot(pick_mask.astype(jnp.float32), numbers).astype(jnp.bfloat16)
-    tags = jnp.broadcast_to(tags.reshape(peers, MOST, 1), (peers, MOST, 128))
-    arriving = lax.all_to_all(
-        jnp.concatenate([outgoing, tags], axis=2), "tensor", split_axis=0, concat_axis=0, tiled=True
-    ).reshape(peers * MOST, width + 128)
-    low = jnp.dot(
-        arriving[:, :width], down_factor_weight[0], preferred_element_type=jnp.float32
-    ).astype(jnp.bfloat16)
-    tag_int = arriving[:, width].astype(jnp.int32)
-    base_row = (jnp.arange(peers * MOST, dtype=jnp.int32) // MOST) * row_count
-    dest = jnp.where(tag_int > 0, base_row + tag_int - 1, -1)[None, :]
-    place = (jnp.arange(peers * row_count, dtype=jnp.int32)[:, None] == dest).astype(jnp.bfloat16)
-    placed = jnp.dot(place, low, preferred_element_type=jnp.float32).astype(jnp.bfloat16)
-    lhs = jnp.concatenate([heads, placed], axis=1)
-    return project_and_sum(lhs, output_projection_weight, up_factor_weight[0], peers)
+    return project_and_sum(
+        attn,
+        target,
+        down_factor_weight[0],
+        output_projection_weight,
+        up_factor_weight[0],
+        peers,
+    )
 
 
 def solution(mesh):

time: 99.7 us -> 88.5 us (0.89)
  Pallas kernels: 55.8 us -> 74.9 us
  starting transfers between devices: 11.4 us -> 0 us
  waiting for transfers between devices: 10.6 us -> 0 us
  local copies, waits for them, and re-layouts: 10.9 us -> 6.5 us
  other arithmetic: 4.29 us -> 1.68 us
    pallas_call x1, Pallas kernels: 55.8 us -> 74.9 us  [project_and_sum(): pl.pallas_call(functools.partial(project_kernel, lines), out_shape=jax.Sh...]
    all_to_all x2 -> x0, starting transfers between devices: 11.4 us -> none  [the longest x1 7.38 us: on_device(): lax.all_to_all(jnp.concatenate([outgoing, tags], axis=2), 'tensor', split...]
    all_to_all x2 -> x0, waiting for transfers between devices: 10.6 us -> none  [the longest x1 5.56 us: on_device(): lax.all_to_all(jnp.concatenate([outgoing, tags], axis=2), 'tensor', split...]
    convert_element_type x3 -> x0, local copies, waits for them, and re-layouts: 3.65 us -> none  [the longest x2 3.53 us: attend(): return summed.reshape(req_count, KVH * per_group * HD).astype(jnp.bfloat16)]
    dot_general x3 -> x0, matrix products: 1.94 us -> none  [the longest x1 1.6 us: on_device(): jnp.dot(place, low, preferred_element_type=jnp.float32).astype(jnp.bfloat16)]
    concatenate x2 -> x0, other arithmetic: 1.8 us -> none  [the longest x1 0.98 us: on_device(): lhs = jnp.concatenate([heads, placed], axis=1)]
    dot_general x1, matrix products: 0.73 us -> 1.86 us  [attend(): jnp.einsum('rkgl,rlkd->rkgd', probs, cached_values, preferred_element_typ...]
    unnamed x16 -> x21, local copies, waits for them, and re-layouts: 5.39 us -> 6.36 us
  transfers between devices with their start and end apart: 2 -> 0, of which waited for: 2 -> 0; matrix products, arithmetic and copies ran while one was open for 7% -> 0% of each run, Pallas kernels for 0% -> 0%
where the time goes in v3:
time: 88.5 us; the launch traced here: 88.3 us
  Pallas kernels  74.9 us (85%)
  local copies, waits for them, and re-layouts  6.5 us (7%)
  matrix products  5.01 us (6%)
  other arithmetic  1.68 us (2%)
    pallas_call x1, Pallas kernels, project_and_sum(): pl.pallas_call(functools.partial(project_kernel, lines), out_shape=jax.Sh...  74.9 us
    unnamed x21, local copies, waits for them, and re-layouts  6.36 us
    dot_general x1, matrix products, attend(): jnp.einsum('rkgd,rlkd->rkgl', query_heads, cached_keys, preferred_element...  2.88 us
    dot_general x1, matrix products, attend(): jnp.einsum('rkgl,rlkd->rkgd', probs, cached_values, preferred_element_typ...  1.86 us

profile of v3, /device:TPU:0, one launch (start us, length us, event | category | flops | bytes accessed | tf_op | source)
XLA Modules:
  0.0 88.3 jit_solution(4405501312002410063)
XLA Ops:
  0.0 0.0 copy-start
  0.0 0.0 copy-start.5
  0.0 0.9 %iota_compare_fusion.1 = pred[32,64]{1,0:T(8,128)(4,1)S(1)} fusion(s32[32]{0:T(128)} %param.16), kind=kLoop, calls=%fused_computation.24 | loop fusion | flops 2048 | bytes 2176 | tf_op jit(solution)/shard_map/lt | solution.py:41
  0.9 1.0 %copy.22 = bf16[4,8,32,128]{3,2,1,0:T(8,128)(2,1)S(1)} copy(bf16[4,8,32,128]{3,1,2,0:T(8,128)(2,1)} %bitcast.51) | data formatting | bytes 524288
  1.9 0.0 copy-start.6
  1.9 2.9 %select_reduce_fusion = (f32[32,4,8]{2,1,0:T(4,128)S(1)}, f32[32,4,8,64]{3,2,1,0:T(8,128)S(1)}) fusion(pred[32,64]{1,0:T(8,128)(4,1)S(1)} %iota_compare_fusion.1, bf16[32,4,8,128]{3,2,1,0:T(8,128)(2,1)S(1)} %bitcast.47, bf16[32,64,512]{2,1,0:T(8,128)(2,1)} %param.14), kind=kOutput, calls=%fused_computation.11 | convolution fusion | flops 16972800 | bytes 2627584 | tf_op jit(solution)/shard_map/rkgd,rlkd->rkgl/dot_general | solution.py:34
  4.8 0.0 copy-start.4
  4.8 0.0 copy-done.5
  4.8 0.3 fusion.26
  5.2 0.4 fusion.15
  5.6 0.1 fusion.22
  5.7 0.0 copy-done.4
  5.7 0.0 copy-done.6
  5.7 0.0 copy-done
  5.7 0.0 copy-start.7
  5.7 0.0 copy-start.8
  5.7 0.0 copy-start.2
  5.8 1.9 %fusion.12 = bf16[32,4,8,128]{3,2,1,0:T(8,128)(2,1)S(1)} fusion(f32[32,4,8,64]{3,2,1,0:T(8,128)} %copy-done.4, f32[32,4,128]{2,1,0:T(4,128)S(1)} %reshape.78, f32[32,4,8]{2,1,0:T(4,128)S(1)} %get-tuple-element.6, f32[32,4,8]{2,1,0:T(4,128)S(1)} %get-tuple-element.5, f32[32,4,8]{2,1,0:T(4,128)S(1)} %multiply_maximum_fusion, ...), kind=kOutput, calls=%fused_computation.8 | convolution fusion | flops 17432576 | bytes 2701312 | tf_op jit(solution)/shard_map/rkgl,rlkd->rkgd/dot_general | solution.py:50
  7.6 0.1 copy.41
  7.7 0.0 copy-done.7
  7.7 0.0 copy-done.8
  7.7 0.1 select_reduce_fusion.1
  7.8 0.2 convert_reduce_fusion
  8.0 0.1 copy.17.target_column_ref
  8.1 0.0 copy-done.2
  8.1 0.0 copy-start.1
  8.1 3.4 %copy-done.1 = bf16[512,8192]{1,0:T(8,128)(2,1)S(1)} copy-done((bf16[512,8192]{1,0:T(8,128)(2,1)S(1)}, bf16[512,8192]{1,0:T(8,128)(2,1)}, u32[]{:S(2)}) %copy-start.1) | copy-done | bytes 8388632
  11.5 0.0 copy-start.3
  11.5 1.0 %copy-done.3 = bf16[1,4096,64]{1,2,0:T(8,128)(2,1)S(1)} copy-done((bf16[1,4096,64]{1,2,0:T(8,128)(2,1)S(1)}, bf16[1,4096,64]{1,2,0:T(8,128)(2,1)}, u32[]{:S(2)}) %copy-start.3) | copy-done | bytes 524312
  12.5 74.9 %shard_map.109 = bf16[32,8192]{1,0:T(8,128)(2,1)S(1)} custom-call(bf16[32,4096]{1,0:T(8,128)(2,1)S(1)} %bitcast.44, s32[1,32]{1,0:T(1,128)S(1)} %get-tuple-element.8.target_row_ref, s32[32,1]{1,0:T(8,128)S(1)} %copy.17.target_column_ref, bf16[64,4096]{1,0:T(8,128)(2,1)S(1)} %bitcast.46, bf16[512,8192]{1,0:T(8,128)(2,1)S(1)} %copy-done.1, ...), custom_call_target="tpu_custom_call" | custom-call | flops 2415919104 | bytes 9437184 | tf_op jit(solution)/shard_map/pallas_call | solution.py:253
  87.5 0.8 copy.43
  (4 shorter events, 0.1 us)
Async XLA Ops:
  0.0 5.7 %copy-start = (bf16[32,64,512]{2,1,0:T(8,128)(2,1)S(1)}, bf16[32,64,512]{2,1,0:T(8,128)(2,1)}, u32[]{:S(2)}) copy-start(bf16[32,64,512]{2,1,0:T(8,128)(2,1)} %param.15) | copy-start | bytes 6291460
  0.0 4.8 %copy-start.5 = (bf16[32,512]{1,0:T(8,128)(2,1)S(1)}, bf16[32,512]{1,0:T(8,128)(2,1)}, u32[]{:S(2)}) copy-start(bf16[32,512]{1,0:T(8,128)(2,1)} %param.12) | copy-start | bytes 98308
  1.9 3.8 %copy-start.6 = (bf16[32,512]{1,0:T(8,128)(2,1)S(1)}, bf16[32,512]{1,0:T(8,128)(2,1)}, u32[]{:S(2)}) copy-start(bf16[32,512]{1,0:T(8,128)(2,1)} %param.13) | copy-start | bytes 98308
  4.8 0.9 copy-start.4
  5.7 2.0 %copy-start.7 = (s32[8]{0:T(128)S(1)}, s32[8]{0:T(128)}, u32[]{:S(2)}) copy-start(s32[8]{0:T(128)} %param.18) | copy-start | bytes 100
  5.7 2.0 %copy-start.8 = (s32[32,1]{0,1:T(1,128)S(1)}, s32[32,1]{0,1:T(1,128)}, u32[]{:S(2)}) copy-start(s32[32,1]{0,1:T(1,128)} %param.17) | copy-start | bytes 388
  5.7 2.4 %copy-start.2 = (bf16[1,64,8192]{2,1,0:T(8,128)(2,1)S(1)}, bf16[1,64,8192]{2,1,0:T(8,128)(2,1)}, u32[]{:S(2)}) copy-start(bf16[1,64,8192]{2,1,0:T(8,128)(2,1)} %param.21) | copy-start | bytes 3145732
  8.1 3.4 %copy-start.1 = (bf16[512,8192]{1,0:T(8,128)(2,1)S(1)}, bf16[512,8192]{1,0:T(8,128)(2,1)}, u32[]{:S(2)}) copy-start(bf16[512,8192]{1,0:T(8,128)(2,1)} %weight_ref.1) | copy-start | bytes 25165828
  11.5 1.0 %copy-start.3 = (bf16[1,4096,64]{1,2,0:T(8,128)(2,1)S(1)}, bf16[1,4096,64]{1,2,0:T(8,128)(2,1)}, u32[]{:S(2)}) copy-start(bf16[1,4096,64]{1,2,0:T(8,128)(2,1)} %param.20) | copy-start | bytes 1572868

commit v4 on v3

--- a/solution.py
+++ b/solution.py
@@ -52,7 +52,7 @@
     return summed.reshape(req_count, KVH * per_group * HD).astype(jnp.bfloat16)
 
 
-CHUNKS = 8
+CHUNKS = 16
 
 
 def project_kernel(
@@ -283,7 +283,7 @@
             dma((CHUNKS, lines - 1)),
         ],
         compiler_params=pltpu.CompilerParams(
-            collective_id=0, has_side_effects=True, vmem_limit_bytes=40 * 1024 * 1024
+            collective_id=0, has_side_effects=True, vmem_limit_bytes=58 * 1024 * 1024
         ),
         cost_estimate=pl.CostEstimate(
             flops=2 * peers * rows * (depth + rank) * width,

time: 88.5 us -> 85.6 us (0.967)
  local copies, waits for them, and re-layouts: 6.5 us -> 4.43 us
  matrix products: 5.01 us -> 3.88 us
    unnamed x21 -> x13, local copies, waits for them, and re-layouts: 6.36 us -> 3.7 us
    dot_general x1, matrix products: 1.86 us -> 0.72 us  [attend(): jnp.einsum('rkgl,rlkd->rkgd', probs, cached_values, preferred_element_typ...]
where the time goes in v4:
time: 85.6 us; the launch traced here: 85.3 us
  Pallas kernels  74.7 us (87%)
  local copies, waits for them, and re-layouts  4.43 us (5%)
  matrix products  3.88 us (5%)
  other arithmetic  2.19 us (3%)
    pallas_call x1, Pallas kernels, project_and_sum(): pl.pallas_call(functools.partial(project_kernel, lines), out_shape=jax.Sh...  74.7 us
    unnamed x13, local copies, waits for them, and re-layouts  3.7 us
    dot_general x1, matrix products, attend(): jnp.einsum('rkgd,rlkd->rkgl', query_heads, cached_keys, preferred_element...  2.88 us

profile of v4, /device:TPU:0, one launch (start us, length us, event | category | flops | bytes accessed | tf_op | source)
XLA Modules:
  0.0 85.3 jit_solution(1831313900489622775)
XLA Ops:
  0.0 0.0 copy-start
  0.0 0.0 copy-start.1
  0.0 0.9 %iota_compare_fusion.1 = pred[32,64]{1,0:T(8,128)(4,1)S(1)} fusion(s32[32]{0:T(128)} %param.16), kind=kLoop, calls=%fused_computation.24 | loop fusion | flops 2048 | bytes 2176 | tf_op jit(solution)/shard_map/lt | solution.py:41
  0.9 1.0 %copy.22 = bf16[4,8,32,128]{3,2,1,0:T(8,128)(2,1)S(1)} copy(bf16[4,8,32,128]{3,1,2,0:T(8,128)(2,1)} %bitcast.51) | data formatting | bytes 524288
  1.9 0.0 copy-start.2
  1.9 2.9 %select_reduce_fusion = (f32[32,4,8]{2,1,0:T(4,128)S(1)}, f32[32,4,8,64]{3,2,1,0:T(8,128)S(1)}) fusion(pred[32,64]{1,0:T(8,128)(4,1)S(1)} %iota_compare_fusion.1, bf16[32,4,8,128]{3,2,1,0:T(8,128)(2,1)S(1)} %bitcast.45, bf16[32,64,512]{2,1,0:T(8,128)(2,1)} %param.14), kind=kOutput, calls=%fused_computation.11 | convolution fusion | flops 16972800 | bytes 2627584 | tf_op jit(solution)/shard_map/rkgd,rlkd->rkgl/dot_general | solution.py:34
  4.8 0.0 copy-done.1
  4.8 0.3 fusion.26
  5.1 0.4 fusion.15
  5.6 0.1 fusion.22
  5.6 0.0 copy-done.2
  5.7 0.0 copy-done
  5.7 0.0 copy-start.3
  5.7 0.0 copy-start.4
  5.7 0.7 fusion.12
  6.5 0.8 copy.41
  7.3 0.0 copy-done.3
  7.3 0.0 copy-done.4
  7.3 0.1 select_reduce_fusion.1
  7.4 0.2 convert_reduce_fusion
  7.5 0.5 fusion.24
  8.0 0.7 copy.17.target_column_ref
  8.7 74.7 %shard_map.109 = bf16[32,8192]{1,0:T(8,128)(2,1)} custom-call(bf16[32,4096]{1,0:T(8,128)(2,1)} %bitcast.44, s32[1,32]{1,0:T(1,128)} %get-tuple-element.8.target_row_ref, s32[32,1]{1,0:T(8,128)} %copy.17.target_column_ref, bf16[64,4096]{1,0:T(8,128)(2,1)} %bitcast.48, bf16[512,8192]{1,0:T(8,128)(2,1)} %weight_ref.1, bf16[64,8192]{1,0:T(8,128)(2,1)} %bitcast.47), custom_call_target="tpu_custom_call" | custom-call | flops 2415919104 | bytes 9437184 | tf_op jit(solution)/shard_map/pallas_call | solution.py:253
  83.4 1.9 %copy.43 = bf16[32,8192]{1,0:T(8,128)(2,1)} copy(bf16[32,8192]{1,0:T(8,128)(2,1)} %shard_map.109) | data formatting | bytes 1048576
  (3 shorter events, 0.1 us)
Async XLA Ops:
  0.0 5.7 %copy-start = (bf16[32,64,512]{2,1,0:T(8,128)(2,1)S(1)}, bf16[32,64,512]{2,1,0:T(8,128)(2,1)}, u32[]{:S(2)}) copy-start(bf16[32,64,512]{2,1,0:T(8,128)(2,1)} %param.15) | copy-start | bytes 6291460
  0.0 4.8 %copy-start.1 = (bf16[32,512]{1,0:T(8,128)(2,1)S(1)}, bf16[32,512]{1,0:T(8,128)(2,1)}, u32[]{:S(2)}) copy-start(bf16[32,512]{1,0:T(8,128)(2,1)} %param.12) | copy-start | bytes 98308
  1.9 3.8 %copy-start.2 = (bf16[32,512]{1,0:T(8,128)(2,1)S(1)}, bf16[32,512]{1,0:T(8,128)(2,1)}, u32[]{:S(2)}) copy-start(bf16[32,512]{1,0:T(8,128)(2,1)} %param.13) | copy-start | bytes 98308
  5.7 1.6 %copy-start.3 = (s32[8]{0:T(128)S(1)}, s32[8]{0:T(128)}, u32[]{:S(2)}) copy-start(s32[8]{0:T(128)} %param.18) | copy-start | bytes 100
  5.7 1.6 %copy-start.4 = (s32[32,1]{0,1:T(1,128)S(1)}, s32[32,1]{0,1:T(1,128)}, u32[]{:S(2)}) copy-start(s32[32,1]{0,1:T(1,128)} %param.17) | copy-start | bytes 388

commit v5 on v4

--- a/solution.py
+++ b/solution.py
@@ -59,11 +59,12 @@
     lines,
     attn_ref,
     target_row_ref,
-    target_column_ref,
     down_ref,
     weight_ref,
     up_ref,
     out_ref,
+    row_outbox,
+    row_inbox,
     outbox,
     inbox,
     lhs_ref,
@@ -107,13 +108,14 @@
             up_ref.at[:, columns(c)], weights.at[c, pl.ds(depth, rank)], up_sem.at[c]
         )
 
-    def mail_copy(k):
+    def mail_copy(kind, k):
         to = (me + k) % peers
+        outgoing, incoming = (row_outbox, row_inbox) if kind == 0 else (outbox, inbox)
         return pltpu.make_async_remote_copy(
-            src_ref=outbox.at[to],
-            dst_ref=inbox.at[me],
-            send_sem=mail_send.at[k - 1],
-            recv_sem=mail_recv.at[k - 1],
+            src_ref=outgoing.at[to],
+            dst_ref=incoming.at[me],
+            send_sem=mail_send.at[kind, k - 1],
+            recv_sem=mail_recv.at[kind, k - 1],
             device_id={"tensor": to},
             device_id_type=pl.DeviceIdType.MESH,
         )
@@ -153,8 +155,6 @@
             device_id_type=pl.DeviceIdType.MESH,
         )
 
-    for p in range(peers):
-        outbox[p, :, :depth] = attn_ref[:, p * depth : (p + 1) * depth]
     picked_shape = (peers * rows, rows)
     spot = lax.broadcasted_iota(jnp.int32, picked_shape, 0)
     wanted = (spot // rows) * MOST + (spot % rows) // blocks
@@ -167,20 +167,29 @@
             attn_ref[:, b * block : (b + 1) * block],
             preferred_element_type=jnp.float32,
         )
-    outbox[:, :, depth : depth + block] = picked.astype(jnp.bfloat16).reshape(peers, rows, block)
-    target = jnp.broadcast_to(target_column_ref[...], (rows, 128))
+    row_outbox[:, :, :block] = picked.astype(jnp.bfloat16).reshape(peers, rows, block)
+    diagonal = lax.broadcasted_iota(jnp.int32, (rows, rows), 0) == lax.broadcasted_iota(
+        jnp.int32, (rows, rows), 1
+    )
+    target = jnp.where(diagonal, jnp.broadcast_to(target_row_ref[...], (rows, rows)), 0)
+    target = jnp.broadcast_to(jnp.sum(target, axis=1, keepdims=True), (rows, 128))
     lane = lax.broadcasted_iota(jnp.int32, (rows, 128), 1)
     for p in range(peers):
         here = (target // MOST == p) & (lane == me * MOST + target % MOST)
-        outbox[p, :, depth + block :] = jnp.where(here, 1.0, 0.0).astype(jnp.bfloat16)
+        row_outbox[p, :, block:] = jnp.where(here, 1.0, 0.0).astype(jnp.bfloat16)
     pl.semaphore_wait(barrier, peers - 1)
     for k in range(1, peers):
-        mail_copy(k).start()
+        mail_copy(0, k).start()
+    for p in range(peers):
+        outbox[p] = attn_ref[:, p * depth : (p + 1) * depth]
+    for k in range(1, peers):
+        mail_copy(1, k).start()
+    row_inbox[me] = row_outbox[me]
     inbox[me] = outbox[me]
     for k in range(1, peers):
-        mail_copy(k).wait_recv()
-
-    arrived = inbox[:, :, depth : depth + block].reshape(peers * rows, block)
+        mail_copy(0, k).wait_recv()
+
+    arrived = row_inbox[:, :, :block].reshape(peers * rows, block)
     spot = lax.broadcasted_iota(jnp.int32, (peers * rows, rank), 0)
     low = jnp.zeros((peers * rows, rank), jnp.float32)
     for b in range(blocks):
@@ -193,11 +202,13 @@
         low = low + jnp.where(spot % blocks == b, term, 0.0)
     low = jnp.sum(low.reshape(peers * MOST, blocks, rank), axis=1)
     low = jnp.concatenate([low, jnp.zeros((128 - peers * MOST, rank), jnp.float32)], axis=0)
-    place = inbox[:, :, depth + block :].reshape(peers * rows, 128)
+    place = row_inbox[:, :, block:].reshape(peers * rows, 128)
     placed = jnp.dot(place, low.astype(jnp.bfloat16), preferred_element_type=jnp.float32)
     placed = placed.astype(jnp.bfloat16).reshape(lines, 2, rows, rank)
-    lhs_ref[:, :, :, :depth] = inbox[:, :, :depth].reshape(lines, 2, rows, depth)
     lhs_ref[:, :, :, depth:] = placed
+    for k in range(1, peers):
+        mail_copy(1, k).wait_recv()
+    lhs_ref[:, :, :, :depth] = inbox[...].reshape(lines, 2, rows, depth)
 
     @pl.loop(0, CHUNKS)
     def _(c):
@@ -239,7 +250,8 @@
             line_copy(c, k).wait_send()
 
     for k in range(1, peers):
-        mail_copy(k).wait_send()
+        mail_copy(0, k).wait_send()
+        mail_copy(1, k).wait_send()
 
 
 def project_and_sum(attn, target, down, weight, up, peers):
@@ -248,13 +260,12 @@
     depth, width = weight.shape
     rank = up.shape[0]
     span = width // CHUNKS
-    letter = depth + MOST * attn.shape[1] // rows + 128
+    letter = MOST * attn.shape[1] // rows + 128
     dma = pltpu.SemaphoreType.DMA
     return pl.pallas_call(
         functools.partial(project_kernel, lines),
         out_shape=jax.ShapeDtypeStruct((rows, width), jnp.bfloat16),
         in_specs=[
-            pl.BlockSpec(memory_space=pltpu.VMEM),
             pl.BlockSpec(memory_space=pltpu.VMEM),
             pl.BlockSpec(memory_space=pltpu.VMEM),
             pl.BlockSpec(memory_space=pltpu.VMEM),
@@ -265,6 +276,8 @@
         scratch_shapes=[
             pltpu.VMEM((peers, rows, letter), jnp.bfloat16),
             pltpu.VMEM((peers, rows, letter), jnp.bfloat16),
+            pltpu.VMEM((peers, rows, depth), jnp.bfloat16),
+            pltpu.VMEM((peers, rows, depth), jnp.bfloat16),
             pltpu.VMEM((lines, 2, rows, depth + rank), jnp.bfloat16),
             pltpu.VMEM((CHUNKS, depth + rank, span), jnp.bfloat16),
             pltpu.VMEM((CHUNKS, lines, rows, span), jnp.bfloat16),
@@ -273,8 +286,8 @@
             pltpu.VMEM((CHUNKS, lines - 1, rows, span), jnp.bfloat16),
             pltpu.VMEM((lines, rows, span), jnp.float32),
             pltpu.VMEM((CHUNKS, rows, span), jnp.float32),
-            dma((peers - 1,)),
-            dma((peers - 1,)),
+            dma((2, peers - 1)),
+            dma((2, peers - 1)),
             dma((CHUNKS,)),
             dma((CHUNKS,)),
             dma((CHUNKS,)),
@@ -290,7 +303,7 @@
             bytes_accessed=2 * (depth + rank) * width,
             transcendentals=0,
         ),
-    )(attn, target.reshape(1, rows), target.reshape(rows, 1), down.T, weight, up)
+    )(attn, target.reshape(1, rows), down.T, weight, up)
 
 
 def on_device(

time: 85.6 us -> 84.2 us (0.984)
  no operation moved by 1% of the time
where the time goes in v5:
time: 84.2 us; the launch traced here: 84 us
  Pallas kernels  74 us (88%)
  matrix products  3.88 us (5%)
  local copies, waits for them, and re-layouts  3.74 us (4%)
  other arithmetic  2.28 us (3%)
    pallas_call x1, Pallas kernels, project_and_sum(): pl.pallas_call(functools.partial(project_kernel, lines), out_shape=jax.Sh...  74 us
    unnamed x13, local copies, waits for them, and re-layouts  3.7 us
    dot_general x1, matrix products, attend(): jnp.einsum('rkgd,rlkd->rkgl', query_heads, cached_keys, preferred_element...  2.88 us

profile of v5, /device:TPU:0, one launch (start us, length us, event | category | flops | bytes accessed | tf_op | source)
XLA Modules:
  0.0 84.0 jit_solution(3407576540085528722)
XLA Ops:
  0.0 0.0 copy-start
  0.0 0.0 copy-start.1
  0.0 0.9 %iota_compare_fusion.1 = pred[32,64]{1,0:T(8,128)(4,1)S(1)} fusion(s32[32]{0:T(128)} %param.16), kind=kLoop, calls=%fused_computation.24 | loop fusion | flops 2048 | bytes 2176 | tf_op jit(solution)/shard_map/lt | solution.py:41
  0.9 1.0 %copy.20 = bf16[4,8,32,128]{3,2,1,0:T(8,128)(2,1)S(1)} copy(bf16[4,8,32,128]{3,1,2,0:T(8,128)(2,1)} %bitcast.49) | data formatting | bytes 524288
  1.9 0.0 copy-start.2
  1.9 2.9 %select_reduce_fusion = (f32[32,4,8]{2,1,0:T(4,128)S(1)}, f32[32,4,8,64]{3,2,1,0:T(8,128)S(1)}) fusion(pred[32,64]{1,0:T(8,128)(4,1)S(1)} %iota_compare_fusion.1, bf16[32,4,8,128]{3,2,1,0:T(8,128)(2,1)S(1)} %bitcast.43, bf16[32,64,512]{2,1,0:T(8,128)(2,1)} %param.14), kind=kOutput, calls=%fused_computation.11 | convolution fusion | flops 16972800 | bytes 2627584 | tf_op jit(solution)/shard_map/rkgd,rlkd->rkgl/dot_general | solution.py:34
  4.8 0.0 copy-done.1
  4.8 0.3 fusion.24
  5.1 0.4 fusion.15
  5.6 0.1 fusion.22
  5.6 0.0 copy-done.2
  5.7 0.0 copy-done
  5.7 0.0 copy-start.3
  5.7 0.0 copy-start.4
  5.7 0.7 fusion.12
  6.5 0.8 copy.39
  7.3 0.0 copy-done.3
  7.3 0.0 copy-done.4
  7.3 0.1 select_reduce_fusion.1
  7.4 0.2 convert_reduce_fusion
  7.5 0.6 add_bitcast_fusion.target_row_ref
  8.1 74.0 %shard_map.109 = bf16[32,8192]{1,0:T(8,128)(2,1)} custom-call(bf16[32,4096]{1,0:T(8,128)(2,1)} %bitcast.42, s32[1,32]{1,0:T(1,128)} %add_bitcast_fusion.target_row_ref, bf16[64,4096]{1,0:T(8,128)(2,1)} %bitcast.46, bf16[512,8192]{1,0:T(8,128)(2,1)} %weight_ref.1, bf16[64,8192]{1,0:T(8,128)(2,1)} %bitcast.45), custom_call_target="tpu_custom_call" | custom-call | flops 2415919104 | bytes 9437184 | tf_op jit(solution)/shard_map/pallas_call | solution.py:265
  82.1 1.9 %copy.41 = bf16[32,8192]{1,0:T(8,128)(2,1)} copy(bf16[32,8192]{1,0:T(8,128)(2,1)} %shard_map.109) | data formatting | bytes 1048576
  (3 shorter events, 0.1 us)
Async XLA Ops:
  0.0 5.7 %copy-start = (bf16[32,64,512]{2,1,0:T(8,128)(2,1)S(1)}, bf16[32,64,512]{2,1,0:T(8,128)(2,1)}, u32[]{:S(2)}) copy-start(bf16[32,64,512]{2,1,0:T(8,128)(2,1)} %param.15) | copy-start | bytes 6291460
  0.0 4.8 %copy-start.1 = (bf16[32,512]{1,0:T(8,128)(2,1)S(1)}, bf16[32,512]{1,0:T(8,128)(2,1)}, u32[]{:S(2)}) copy-start(bf16[32,512]{1,0:T(8,128)(2,1)} %param.12) | copy-start | bytes 98308
  1.9 3.8 %copy-start.2 = (bf16[32,512]{1,0:T(8,128)(2,1)S(1)}, bf16[32,512]{1,0:T(8,128)(2,1)}, u32[]{:S(2)}) copy-start(bf16[32,512]{1,0:T(8,128)(2,1)} %param.13) | copy-start | bytes 98308
  5.7 1.6 %copy-start.3 = (s32[8]{0:T(128)S(1)}, s32[8]{0:T(128)}, u32[]{:S(2)}) copy-start(s32[8]{0:T(128)} %param.18) | copy-start | bytes 100
  5.7 1.6 %copy-start.4 = (s32[32,1]{0,1:T(1,128)S(1)}, s32[32,1]{0,1:T(1,128)}, u32[]{:S(2)}) copy-start(s32[32,1]{0,1:T(1,128)} %param.17) | copy-start | bytes 388

commit v6 on v5

--- a/solution.py
+++ b/solution.py
@@ -71,6 +71,8 @@
     weights,
     pair_out,
     pair_in,
+    near_out,
+    near_in,
     line_out,
     line_in,
     own,
@@ -81,11 +83,15 @@
     up_sem,
     pair_send,
     pair_recv,
+    near_send,
+    near_recv,
     line_send,
     line_recv,
 ):
     me = lax.axis_index("tensor")
     line, side = me // 2, me % 2
+    half, parity = line // 2, line % 2
+    halves = lines // 2
     other = 2 * line + (1 - side)
     depth = weight_ref.shape[0]
     rank = up_ref.shape[0]
@@ -130,10 +136,20 @@
             device_id_type=pl.DeviceIdType.MESH,
         )
 
+    def near_copy(c):
+        return pltpu.make_async_remote_copy(
+            src_ref=near_out.at[c],
+            dst_ref=near_in.at[c],
+            send_sem=near_send.at[c],
+            recv_sem=near_recv.at[c],
+            device_id={"tensor": 2 * (2 * half + 1 - parity) + side},
+            device_id_type=pl.DeviceIdType.MESH,
+        )
+
     def line_copy(c, k):
-        to = (line + k) % lines
+        to = 2 * ((half + k) % halves) + parity
         return pltpu.make_async_remote_copy(
-            src_ref=line_out.at[c, k],
+            src_ref=line_out.at[c, k - 1],
             dst_ref=line_in.at[c, k - 1],
             send_sem=line_send.at[c, k - 1],
             recv_sem=line_recv.at[c, k - 1],
@@ -226,19 +242,28 @@
         pair_own = part.reshape(lines, rows, span)
         own[...] = pair_own
         pair_copy(c).wait_recv()
-        for k in range(lines):
-            to = (line + k) % lines
+        for i in range(halves):
+            to = 2 * i + 1 - parity
             both = own[to] + pair_in[c, to].astype(jnp.float32)
-            if k == 0:
-                kept[c] = both
-            else:
-                line_out[c, k] = both.astype(jnp.bfloat16)
-                line_copy(c, k).start()
-
-    @pl.loop(0, CHUNKS)
-    def _(c):
-        total = kept[c]
-        for k in range(1, lines):
+            near_out[c, i] = both.astype(jnp.bfloat16)
+        near_copy(c).start()
+        for i in range(halves):
+            to = 2 * i + parity
+            kept[c, i] = own[to] + pair_in[c, to].astype(jnp.float32)
+
+    @pl.loop(0, CHUNKS)
+    def _(c):
+        near_copy(c).wait_recv()
+        for k in range(1, halves):
+            i = (half + k) % halves
+            both = kept[c, i] + near_in[c, i].astype(jnp.float32)
+            line_out[c, k - 1] = both.astype(jnp.bfloat16)
+            line_copy(c, k).start()
+
+    @pl.loop(0, CHUNKS)
+    def _(c):
+        total = kept[c, half] + near_in[c, half].astype(jnp.float32)
+        for k in range(1, halves):
             line_copy(c, k).wait_recv()
             total = total + line_in[c, k - 1].astype(jnp.float32)
         out_ref[:, columns(c)] = total.astype(jnp.bfloat16)
@@ -246,7 +271,8 @@
     @pl.loop(0, CHUNKS)
     def _(c):
         pair_copy(c).wait_send()
-        for k in range(1, lines):
+        near_copy(c).wait_send()
+        for k in range(1, halves):
             line_copy(c, k).wait_send()
 
     for k in range(1, peers):
@@ -282,18 +308,22 @@
             pltpu.VMEM((CHUNKS, depth + rank, span), jnp.bfloat16),
             pltpu.VMEM((CHUNKS, lines, rows, span), jnp.bfloat16),
             pltpu.VMEM((CHUNKS, lines, rows, span), jnp.bfloat16),
-            pltpu.VMEM((CHUNKS, lines, rows, span), jnp.bfloat16),
-            pltpu.VMEM((CHUNKS, lines - 1, rows, span), jnp.bfloat16),
+            pltpu.VMEM((CHUNKS, lines // 2, rows, span), jnp.bfloat16),
+            pltpu.VMEM((CHUNKS, lines // 2, rows, span), jnp.bfloat16),
+            pltpu.VMEM((CHUNKS, lines // 2 - 1, rows, span), jnp.bfloat16),
+            pltpu.VMEM((CHUNKS, lines // 2 - 1, rows, span), jnp.bfloat16),
             pltpu.VMEM((lines, rows, span), jnp.float32),
-            pltpu.VMEM((CHUNKS, rows, span), jnp.float32),
+            pltpu.VMEM((CHUNKS, lines // 2, rows, span), jnp.float32),
             dma((2, peers - 1)),
             dma((2, peers - 1)),
             dma((CHUNKS,)),
             dma((CHUNKS,)),
             dma((CHUNKS,)),
             dma((CHUNKS,)),
-            dma((CHUNKS, lines - 1)),
-            dma((CHUNKS, lines - 1)),
+            dma((CHUNKS,)),
+            dma((CHUNKS,)),
+            dma((CHUNKS, lines // 2 - 1)),
+            dma((CHUNKS, lines // 2 - 1)),
         ],
         compiler_params=pltpu.CompilerParams(
             collective_id=0, has_side_effects=True, vmem_limit_bytes=58 * 1024 * 1024

time: 84.2 us -> 102 us (1.21)
  the two profiles are of different devices: /device:TPU:0 before, /device:TPU:24 now
where the time goes in v6:
time: 102 us; the launch traced here: 101 us
  Pallas kernels  91.5 us (90%)
  matrix products  3.88 us (4%)
  local copies, waits for them, and re-layouts  3.74 us (4%)
  other arithmetic  2.28 us (2%)
    pallas_call x1, Pallas kernels, project_and_sum(): pl.pallas_call(functools.partial(project_kernel, lines), out_shape=jax.Sh...  91.5 us
    unnamed x13, local copies, waits for them, and re-layouts  3.7 us
    dot_general x1, matrix products, attend(): jnp.einsum('rkgd,rlkd->rkgl', query_heads, cached_keys, preferred_element...  2.88 us

profile of v6, /device:TPU:24, one launch (start us, length us, event | category | flops | bytes accessed | tf_op | source)
XLA Modules:
  0.0 101.5 jit_solution(14966916141091959989)
XLA Ops:
  0.0 0.0 copy-start
  0.0 0.0 copy-start.1
  0.0 0.9 iota_compare_fusion.1
  0.9 1.0 copy.20
  1.9 0.0 copy-start.2
  1.9 2.9 %select_reduce_fusion = (f32[32,4,8]{2,1,0:T(4,128)S(1)}, f32[32,4,8,64]{3,2,1,0:T(8,128)S(1)}) fusion(pred[32,64]{1,0:T(8,128)(4,1)S(1)} %iota_compare_fusion.1, bf16[32,4,8,128]{3,2,1,0:T(8,128)(2,1)S(1)} %bitcast.43, bf16[32,64,512]{2,1,0:T(8,128)(2,1)} %param.14), kind=kOutput, calls=%fused_computation.11 | convolution fusion | flops 16972800 | bytes 2627584 | tf_op jit(solution)/shard_map/rkgd,rlkd->rkgl/dot_general | solution.py:34
  4.8 0.0 copy-done.1
  4.8 0.3 fusion.24
  5.1 0.4 fusion.15
  5.6 0.1 fusion.22
  5.6 0.0 copy-done.2
  5.7 0.0 copy-done
  5.7 0.0 copy-start.3
  5.7 0.0 copy-start.4
  5.7 0.7 fusion.12
  6.4 0.8 copy.39
  7.3 0.0 copy-done.3
  7.3 0.0 copy-done.4
  7.3 0.1 select_reduce_fusion.1
  7.4 0.2 convert_reduce_fusion
  7.5 0.6 add_bitcast_fusion.target_row_ref
  8.1 91.5 %shard_map.109 = bf16[32,8192]{1,0:T(8,128)(2,1)} custom-call(bf16[32,4096]{1,0:T(8,128)(2,1)} %bitcast.42, s32[1,32]{1,0:T(1,128)} %add_bitcast_fusion.target_row_ref, bf16[64,4096]{1,0:T(8,128)(2,1)} %bitcast.46, bf16[512,8192]{1,0:T(8,128)(2,1)} %weight_ref.1, bf16[64,8192]{1,0:T(8,128)(2,1)} %bitcast.45), custom_call_target="tpu_custom_call" | custom-call | flops 2415919104 | bytes 9437184 | tf_op jit(solution)/shard_map/pallas_call | solution.py:291
  99.6 1.9 %copy.41 = bf16[32,8192]{1,0:T(8,128)(2,1)} copy(bf16[32,8192]{1,0:T(8,128)(2,1)} %shard_map.109) | data formatting | bytes 1048576
  (3 shorter events, 0.1 us)
Async XLA Ops:
  0.0 5.7 %copy-start = (bf16[32,64,512]{2,1,0:T(8,128)(2,1)S(1)}, bf16[32,64,512]{2,1,0:T(8,128)(2,1)}, u32[]{:S(2)}) copy-start(bf16[32,64,512]{2,1,0:T(8,128)(2,1)} %param.15) | copy-start | bytes 6291460
  0.0 4.8 %copy-start.1 = (bf16[32,512]{1,0:T(8,128)(2,1)S(1)}, bf16[32,512]{1,0:T(8,128)(2,1)}, u32[]{:S(2)}) copy-start(bf16[32,512]{1,0:T(8,128)(2,1)} %param.12) | copy-start | bytes 98308
  1.9 3.8 %copy-start.2 = (bf16[32,512]{1,0:T(8,128)(2,1)S(1)}, bf16[32,512]{1,0:T(8,128)(2,1)}, u32[]{:S(2)}) copy-start(bf16[32,512]{1,0:T(8,128)(2,1)} %param.13) | copy-start | bytes 98308
  5.7 1.6 %copy-start.3 = (s32[8]{0:T(128)S(1)}, s32[8]{0:T(128)}, u32[]{:S(2)}) copy-start(s32[8]{0:T(128)} %param.18) | copy-start | bytes 100
  5.7 1.6 %copy-start.4 = (s32[32,1]{0,1:T(1,128)S(1)}, s32[32,1]{0,1:T(1,128)}, u32[]{:S(2)}) copy-start(s32[32,1]{0,1:T(1,128)} %param.17) | copy-start | bytes 388

commit v7 on v6

--- a/solution.py
+++ b/solution.py
@@ -235,6 +235,14 @@
         pair_out[c] = part.astype(jnp.bfloat16).reshape(lines, rows, span)
         pair_copy(c).start()
 
+    def far_step(c):
+        near_copy(c).wait_recv()
+        for k in range(1, halves):
+            i = (half + k) % halves
+            both = kept[c, i] + near_in[c, i].astype(jnp.float32)
+            line_out[c, k - 1] = both.astype(jnp.bfloat16)
+            line_copy(c, k).start()
+
     @pl.loop(0, CHUNKS)
     def _(c):
         left = lhs_ref[:, side].reshape(lines * rows, depth + rank)
@@ -251,14 +259,12 @@
             to = 2 * i + parity
             kept[c, i] = own[to] + pair_in[c, to].astype(jnp.float32)
 
-    @pl.loop(0, CHUNKS)
-    def _(c):
-        near_copy(c).wait_recv()
-        for k in range(1, halves):
-            i = (half + k) % halves
-            both = kept[c, i] + near_in[c, i].astype(jnp.float32)
-            line_out[c, k - 1] = both.astype(jnp.bfloat16)
-            line_copy(c, k).start()
+        @pl.when(c >= 2)
+        def _():
+            far_step(c - 2)
+
+    far_step(CHUNKS - 2)
+    far_step(CHUNKS - 1)
 
     @pl.loop(0, CHUNKS)
     def _(c):

time: 102 us -> 87.1 us (0.85)
  the two profiles are of different devices: /device:TPU:24 before, /device:TPU:0 now
where the time goes in v7:
time: 87.1 us; the launch traced here: 86.8 us
  Pallas kernels  76.8 us (88%)
  matrix products  3.88 us (4%)
  local copies, waits for them, and re-layouts  3.74 us (4%)
  other arithmetic  2.28 us (3%)
    pallas_call x1, Pallas kernels, project_and_sum(): pl.pallas_call(functools.partial(project_kernel, lines), out_shape=jax.Sh...  76.8 us
    unnamed x13, local copies, waits for them, and re-layouts  3.7 us
    dot_general x1, matrix products, attend(): jnp.einsum('rkgd,rlkd->rkgl', query_heads, cached_keys, preferred_element...  2.88 us

profile of v7, /device:TPU:0, one launch (start us, length us, event | category | flops | bytes accessed | tf_op | source)
XLA Modules:
  0.0 86.8 jit_solution(6760104721489338646)
XLA Ops:
  0.0 0.0 copy-start
  0.0 0.0 copy-start.1
  0.0 0.9 %iota_compare_fusion.1 = pred[32,64]{1,0:T(8,128)(4,1)S(1)} fusion(s32[32]{0:T(128)} %param.16), kind=kLoop, calls=%fused_computation.24 | loop fusion | flops 2048 | bytes 2176 | tf_op jit(solution)/shard_map/lt | solution.py:41
  0.9 1.0 %copy.20 = bf16[4,8,32,128]{3,2,1,0:T(8,128)(2,1)S(1)} copy(bf16[4,8,32,128]{3,1,2,0:T(8,128)(2,1)} %bitcast.49) | data formatting | bytes 524288
  1.9 0.0 copy-start.2
  1.9 2.9 %select_reduce_fusion = (f32[32,4,8]{2,1,0:T(4,128)S(1)}, f32[32,4,8,64]{3,2,1,0:T(8,128)S(1)}) fusion(pred[32,64]{1,0:T(8,128)(4,1)S(1)} %iota_compare_fusion.1, bf16[32,4,8,128]{3,2,1,0:T(8,128)(2,1)S(1)} %bitcast.43, bf16[32,64,512]{2,1,0:T(8,128)(2,1)} %param.14), kind=kOutput, calls=%fused_computation.11 | convolution fusion | flops 16972800 | bytes 2627584 | tf_op jit(solution)/shard_map/rkgd,rlkd->rkgl/dot_general | solution.py:34
  4.8 0.0 copy-done.1
  4.8 0.3 fusion.24
  5.1 0.4 fusion.15
  5.6 0.1 fusion.22
  5.6 0.0 copy-done.2
  5.7 0.0 copy-done
  5.7 0.0 copy-start.3
  5.7 0.0 copy-start.4
  5.7 0.7 fusion.12
  6.5 0.8 copy.39
  7.3 0.0 copy-done.3
  7.3 0.0 copy-done.4
  7.3 0.1 select_reduce_fusion.1
  7.4 0.2 convert_reduce_fusion
  7.5 0.6 add_bitcast_fusion.target_row_ref
  8.1 76.8 %shard_map.109 = bf16[32,8192]{1,0:T(8,128)(2,1)} custom-call(bf16[32,4096]{1,0:T(8,128)(2,1)} %bitcast.42, s32[1,32]{1,0:T(1,128)} %add_bitcast_fusion.target_row_ref, bf16[64,4096]{1,0:T(8,128)(2,1)} %bitcast.46, bf16[512,8192]{1,0:T(8,128)(2,1)} %weight_ref.1, bf16[64,8192]{1,0:T(8,128)(2,1)} %bitcast.45), custom_call_target="tpu_custom_call" | custom-call | flops 2415919104 | bytes 9437184 | tf_op jit(solution)/shard_map/pallas_call | solution.py:297
  85.0 1.9 %copy.41 = bf16[32,8192]{1,0:T(8,128)(2,1)} copy(bf16[32,8192]{1,0:T(8,128)(2,1)} %shard_map.109) | data formatting | bytes 1048576
  (3 shorter events, 0.1 us)
Async XLA Ops:
  0.0 5.7 %copy-start = (bf16[32,64,512]{2,1,0:T(8,128)(2,1)S(1)}, bf16[32,64,512]{2,1,0:T(8,128)(2,1)}, u32[]{:S(2)}) copy-start(bf16[32,64,512]{2,1,0:T(8,128)(2,1)} %param.15) | copy-start | bytes 6291460
  0.0 4.8 %copy-start.1 = (bf16[32,512]{1,0:T(8,128)(2,1)S(1)}, bf16[32,512]{1,0:T(8,128)(2,1)}, u32[]{:S(2)}) copy-start(bf16[32,512]{1,0:T(8,128)(2,1)} %param.12) | copy-start | bytes 98308
  1.9 3.8 %copy-start.2 = (bf16[32,512]{1,0:T(8,128)(2,1)S(1)}, bf16[32,512]{1,0:T(8,128)(2,1)}, u32[]{:S(2)}) copy-start(bf16[32,512]{1,0:T(8,128)(2,1)} %param.13) | copy-start | bytes 98308
  5.7 1.6 %copy-start.3 = (s32[8]{0:T(128)S(1)}, s32[8]{0:T(128)}, u32[]{:S(2)}) copy-start(s32[8]{0:T(128)} %param.18) | copy-start | bytes 100
  5.7 1.6 %copy-start.4 = (s32[32,1]{0,1:T(1,128)S(1)}, s32[32,1]{0,1:T(1,128)}, u32[]{:S(2)}) copy-start(s32[32,1]{0,1:T(1,128)} %param.17) | copy-start | bytes 388
